TPU v7x, 128 devices: a whole 4x4x4 slice. The times are simulated.
128 devices in a mesh: dp: 8 (over z, x_hi), ctx: 16 (over y, x_lo, core).
Axes of the slice: x: 4 (x_hi: 2, x_lo: 2; x = x_hi * 2 + x_lo), y: 4, z: 4, core: 2. Of those that a mesh axis runs over, the one named last changes fastest.
Arguments:
- hidden: bfloat16 [8, 4096, 2048], P('dp', 'ctx'), may hold values from -6 to 6
- x_weight: bfloat16 [2048, 2048], replicated, may hold values from -0.125 to 0.125
- state_weight: bfloat16 [2048, 160], replicated, may hold values from -0.125 to 0.125
- log_rates: float32 [32], replicated, as said below
- step_bias: float32 [32], replicated, may hold values from -1 to 1
- out_gain: float32 [2048], replicated, may hold values from 0.5 to 1.5
- cotangent: bfloat16 [8, 4096, 2048], P('dp', 'ctx'), may hold values from -6 to 6
Outputs:
- mixed: bfloat16 [8, 4096, 2048], P('dp', 'ctx')
- grad_x: float32 [2048, 2048], P('ctx')
- grad_small: float32 [2048, 160], P('ctx')
Inputs may be any that keep to these rules, and one draw needn't show every extreme that they name: Each head's rate exp(log_rates) lies between 0.05 / 4096 and 1 / 30.
All inputs are finite; a program needn't handle non-finite values.
Results may differ from a plain program's by a relative error of at most 0.0049.
Values may be sent and summed in bfloat16 or wider, within the bound.
A program may use at most 192 MiB of HBM per device.

v0:
```python
import jax
import jax.numpy as jnp
from jax import lax
from jax.sharding import PartitionSpec as P

HEAD = 64
STATE = 64


precise = lax.Precision.HIGHEST


def swapped(array, axis, apart):
    return lax.ppermute(array, axis, [(i, i ^ 1 << apart) for i in range(lax.axis_size(axis))])


def carried_in(array, axis, combine, identity, reverse):
    peers, place = (lax.axis_size(axis), lax.axis_index(axis))
    everything = jax.tree.map(lambda part: lax.all_gather(part, axis), array)
    start = jax.tree.map(
        lambda part, zero: jnp.broadcast_to(jnp.asarray(zero, part.dtype), part.shape),
        array,
        identity,
    )

    def step(k, before):
        at = peers - 1 - k if reverse else k
        reached = at > place if reverse else at < place
        new = combine(before, jax.tree.map(lambda part: part[at], everything))
        return jax.tree.map(lambda a, b: jnp.where(reached, a, b), new, before)

    return lax.fori_loop(0, peers, step, start)


def split_small(projected, log_rates, step_bias):
    inputs_b = projected[:, :STATE]
    inputs_c = projected[:, STATE : 2 * STATE]
    step_size = jax.nn.softplus(projected[:, 2 * STATE :] + step_bias[None, :])
    cumlog = jnp.cumsum(-jnp.exp(log_rates)[None, :] * step_size, axis=0)
    return (inputs_b, inputs_c, step_size, cumlog)


def block_state(values_in, projected, log_rates, step_bias):
    inputs_b, inputs_c, step_size, cumlog = split_small(projected, log_rates, step_bias)
    block_rows, channels = values_in.shape
    head_count = channels // HEAD
    per_head = values_in.reshape(block_rows, head_count, HEAD)
    weighting = jnp.exp(cumlog[-1][None, :] - cumlog) * step_size
    local_end = jnp.einsum("sh,shp,sn->hpn", weighting, per_head, inputs_b, precision=precise)
    return (jnp.exp(cumlog[-1]), local_end)


def forward_y(values_in, projected, state_in, log_rates, step_bias, out_gain):
    inputs_b, inputs_c, step_size, cumlog = split_small(projected, log_rates, step_bias)
    block_rows, channels = values_in.shape
    head_count = channels // HEAD
    per_head = values_in.reshape(block_rows, head_count, HEAD)
    log_heads = cumlog.T
    log_gap = log_heads[:, :, None] - log_heads[:, None, :]
    position = jnp.arange(block_rows)
    causal = position[:, None] >= position[None, :]
    decay_mat = jnp.exp(jnp.where(causal[None, :, :], log_gap, -jnp.inf)) * step_size.T[:, None, :]
    scores = jnp.dot(inputs_c, inputs_b.T, precision=precise)
    mixing = decay_mat * scores[None, :, :]
    inner = jnp.einsum("hts,shp->thp", mixing, per_head, precision=precise)
    readout = (
        jnp.einsum("tn,hpn->thp", inputs_c, state_in, precision=precise)
        * jnp.exp(cumlog)[:, :, None]
    )
    unnormed = (inner + readout).reshape(block_rows, channels)
    rescale = lax.rsqrt(jnp.mean(unnormed * unnormed, axis=1, keepdims=True) + 1e-05)
    return unnormed * rescale * out_gain[None, :]


def chain(earlier, later):
    return (earlier[0] * later[0], later[0][:, None, None] * earlier[1] + later[1])


def chain_pair(earlier, later):
    return chain(earlier[:2], later[:2]) + chain(earlier[2:], later[2:])


def contract(left_rows, right_rows):
    return lax.dot_general(
        left_rows, right_rows, (((0,), (0,)), ((), ())), preferred_element_type=jnp.float32
    )


def shards(hidden, x_weight, state_weight, log_rates, step_bias, out_gain, cotangent):
    own_rows = hidden[0]
    own_cot = cotangent[0]
    channels = x_weight.shape[0]
    head_count = channels // HEAD
    unit = (jnp.ones((head_count,), jnp.float32), jnp.zeros((head_count, HEAD, STATE), jnp.float32))
    mirror_steps = lax.axis_size("ctx").bit_length() - 1

    def project(rows_in):
        values = jnp.dot(rows_in, x_weight, preferred_element_type=jnp.float32).astype(jnp.bfloat16)
        projected = jnp.dot(rows_in, state_weight, preferred_element_type=jnp.float32)
        return (values.astype(jnp.float32), projected)

    def local_state(values_in, projected):
        return block_state(values_in, projected, log_rates, step_bias)

    def local_output(values_in, projected, state_in):
        return forward_y(values_in, projected, state_in, log_rates, step_bias, out_gain)

    own_rc_rows = own_rows[::-1, ::-1]
    parcel = jnp.stack([own_rc_rows, own_cot])
    for bit_index in range(mirror_steps):
        parcel = swapped(parcel, "ctx", bit_index)
    rows_rc = parcel[0]
    cot_rc = parcel[1][::-1, ::-1].astype(jnp.float32)
    cot_fwd = own_cot.astype(jnp.float32)
    values_fwd, proj_fwd = project(own_rows)
    values_rc, proj_rc = project(rows_rc)
    (total_fwd, end_fwd), state_back_fwd = jax.vjp(local_state, values_fwd, proj_fwd)
    (total_rc, end_rc), state_back_rc = jax.vjp(local_state, values_rc, proj_rc)
    carried = carried_in(
        (total_fwd, end_fwd, total_rc, end_rc), "ctx", chain_pair, unit + unit, False
    )
    start_fwd = carried[1]
    start_rc = carried[3]
    y_fwd, out_back_fwd = jax.vjp(local_output, values_fwd, proj_fwd, start_fwd)
    y_rc, out_back_rc = jax.vjp(local_output, values_rc, proj_rc, start_rc)
    returned = y_rc.astype(jnp.bfloat16)
    for bit_index in range(mirror_steps):
        returned = swapped(returned, "ctx", bit_index)
    mixed = (y_fwd + returned[::-1, ::-1].astype(jnp.float32)).astype(jnp.bfloat16)
    dval_fwd, dproj_fwd, local_fwd = out_back_fwd(cot_fwd)
    dval_rc, dproj_rc, local_rc = out_back_rc(cot_rc)
    adjoints = carried_in(
        (total_fwd, local_fwd, total_rc, local_rc), "ctx", chain_pair, unit + unit, True
    )
    after_fwd = adjoints[1]
    after_rc = adjoints[3]

    def finish(state_back, dval_first, dproj_first, state_in, after_end):
        dtotal = jnp.sum(after_end * state_in, axis=(1, 2))
        dval_second, dproj_second = state_back((dtotal, after_end))
        return (
            (dval_first + dval_second).astype(jnp.bfloat16),
            (dproj_first + dproj_second).astype(jnp.bfloat16),
        )

    grad_vf, grad_pf = finish(state_back_fwd, dval_fwd, dproj_fwd, start_fwd, after_fwd)
    grad_vr, grad_pr = finish(state_back_rc, dval_rc, dproj_rc, start_rc, after_rc)
    term_x = contract(own_rows, grad_vf) + contract(rows_rc, grad_vr)
    term_small = contract(own_rows, grad_pf) + contract(rows_rc, grad_pr)
    shard_x, shard_small = (
        lax.psum_scatter(term_x, "ctx", scatter_dimension=0, tiled=True),
        lax.psum_scatter(term_small, "ctx", scatter_dimension=0, tiled=True),
    )
    grad_x, grad_small = lax.psum((shard_x, shard_small), "dp")
    return (mixed[None], grad_x, grad_small)


def solution(mesh):
    return jax.shard_map(
        shards,
        mesh=mesh,
        in_specs=(P("dp", "ctx", None), P(), P(), P(), P(), P(), P("dp", "ctx", None)),
        out_specs=(P("dp", "ctx", None), P("ctx", None), P("ctx", None)),
        check_vma=False,
    )
```

profile of v0, /device:TPU:0, one launch (start us, length us, event | category | flops | bytes accessed | tf_op | source)
XLA Modules:
  0.0 1089.9 jit_solution(158915750018869959)
XLA Ops:
  7.2 16.5 %rev.9 = bf16[256,2048]{1,0:T(8,128)(2,1)} reverse(bf16[256,2048]{1,0:T(8,128)(2,1)} %bitcast.344), dimensions={0,1} | reverse | bytes 2097152 | tf_op jit(solution)/shard_map/rev | solution.py:108
  25.3 4.1 collective-permute-done
  31.0 46.1 %collective-permute-done.1 = bf16[2,256,2048]{2,1,0:T(8,128)(2,1)S(1)} collective-permute-done((bf16[2,256,2048]{2,1,0:T(8,128)(2,1)S(1)}, bf16[2,256,2048]{2,1,0:T(8,128)(2,1)S(1)}, u32[]{:S(2)}, u32[]{:S(2)}) %collective-permute-start.1) | collective-permute-done | bytes 2097184 | tf_op jit(solution)/shard_map/ppermute | solution.py:14
  78.8 45.3 %collective-permute-done.2 = bf16[2,256,2048]{2,1,0:T(8,128)(2,1)} collective-permute-done((bf16[2,256,2048]{2,1,0:T(8,128)(2,1)S(1)}, bf16[2,256,2048]{2,1,0:T(8,128)(2,1)}, u32[]{:S(2)}, u32[]{:S(2)}) %collective-permute-start.2) | collective-permute-done | bytes 2097184 | tf_op jit(solution)/shard_map/ppermute | solution.py:14
  127.4 6.7 convolution_convert_fusion.1
  136.1 35.7 %collective-permute-done.3 = bf16[2,256,2048]{2,1,0:T(8,128)(2,1)} collective-permute-done((bf16[2,256,2048]{2,1,0:T(8,128)(2,1)}, bf16[2,256,2048]{2,1,0:T(8,128)(2,1)}, u32[]{:S(2)}, u32[]{:S(2)}) %collective-permute-start.3) | collective-permute-done | bytes 2097184 | tf_op jit(solution)/shard_map/ppermute | solution.py:14
  180.8 6.1 convolution_convert_fusion
  198.3 25.3 %all-gather.4 = f32[16,1,32]{2,1,0:T(1,128)} all-gather(f32[1,1,32]{2,1,0:T(1,128)} %bitcast.366), channel_id=1, replica_groups=mesh['dp'=8,'ctx'=16] {'ctx'}, dimensions={0}, use_global_device_ids=true | all-gather | bytes 2176 | tf_op jit(solution)/shard_map/all_gather | solution.py:19
  223.6 20.5 %all-gather.5 = f32[16,1,32]{2,1,0:T(1,128)} all-gather(f32[1,1,32]{2,1,0:T(1,128)} %bitcast.367), channel_id=1, replica_groups=mesh['dp'=8,'ctx'=16] {'ctx'}, dimensions={0}, use_global_device_ids=true | all-gather | bytes 2176 | tf_op jit(solution)/shard_map/all_gather | solution.py:19
  244.1 30.0 %all-gather.11.cloned.1.call-done = f32[512,64,64]{2,1,0:T(8,128)} async-done(((f32[32,64,64]{2,1,0:T(8,128)}), f32[512,64,64]{2,1,0:T(8,128)}) %all-gather.11.cloned.1.call-update) | async-done | bytes 8388624 | tf_op jit(solution)/shard_map/all_gather | solution.py:19
  274.2 94.9 %all-gather.13.cloned.1.call-done = f32[512,64,64]{2,1,0:T(8,128)} async-done(((f32[32,64,64]{2,1,0:T(8,128)}), f32[512,64,64]{2,1,0:T(8,128)}) %all-gather.13.cloned.1.call-update) | async-done | bytes 8388624 | tf_op jit(solution)/shard_map/all_gather | solution.py:19
  369.0 61.2 %while.34 = (s32[]{:T(128)}, f32[32,64,64]{2,1,0:T(8,128)S(1)}, f32[32,64,64]{2,1,0:T(8,128)S(1)}, s32[]{:T(128)}, f32[16,32]{1,0:T(8,128)}, /*index=5*/f32[16,3...) while((s32[]{:T(128)}, f32[32,64,64]{2,1,0:T(8,128)S(1)}, ...), condition=%wide.region_5.7_spmd.clone, body=%wide.region_4.6_spmd.clone.sunk | while | flops 1048580 | bytes 3146637 | solution.py:32
  432.2 6.3 multiply_reduce_fusion.7
  446.7 13.9 %rev.11 = bf16[256,2048]{1,0:T(8,128)(2,1)S(1)} reverse(bf16[256,2048]{1,0:T(8,128)(2,1)} %slice_bitcast_fusion), dimensions={0,1} | reverse | bytes 2097152 | tf_op jit(solution)/shard_map/rev | solution.py:113
  463.0 8.3 multiply_reduce_fusion.8
  482.3 4.4 fusion.61
  486.9 5.6 fusion.56
  492.6 14.2 %fusion.23 = (f32[32,256]{1,0:T(8,128)}, f32[32,256]{1,0:T(8,128)}, f32[32,256]{1,0:T(8,128)}, f32[256,256]{1,0:T(8,128)}, f32[256,256]{1,0:T(8,128)}, /*index=5...) fusion(f32[256,256]{1,0:T(8,128)S(1)} %copy-done.47, f32[32,256]{1,0:T(8,128)S(1)} %copy-done.73, ...), kind=kOutput, calls=%fused_computation.36 | convolution fusion | flops 1664958464 | bytes 12976128 | tf_op jit(solution)/shard_map/transpose(jvp(hts,shp->thp))/dot_general | solution.py:65
  507.5 3.8 reduce-window.46
  518.8 3.8 reduce-window.54
  536.7 94.1 %all-gather.17.cloned.1.call-done = f32[512,64,64]{2,1,0:T(8,128)} async-done(((f32[32,64,64]{2,1,0:T(8,128)}), f32[512,64,64]{2,1,0:T(8,128)}) %all-gather.17.cloned.1.call-update) | async-done | bytes 8388624 | tf_op jit(solution)/shard_map/all_gather | solution.py:19
  630.9 79.8 %while.35 = (s32[]{:T(128)}, f32[32,64,64]{2,1,0:T(8,128)S(1)}, f32[32,64,64]{2,1,0:T(8,128)}, s32[]{:T(128)}, f32[16,32]{1,0:T(8,128)}, /*index=5*/f32[16,32,64...) while((s32[]{:T(128)}, f32[32,64,64]{2,1,0:T(8,128)S(1)}, ...), condition=%wide.region_11.13_spmd.clone, body=%wide.region_10.12_spmd.clone.sunk | while | flops 1048584 | bytes 3146699 | solution.py:32
  710.6 4.5 fusion.52
  735.9 9.2 fusion.55
  745.2 7.7 fusion.54
  755.3 9.3 bitcast_add_fusion.4
  769.8 29.9 %collective-permute-done.5 = bf16[256,2048]{1,0:T(8,128)(2,1)S(1)} collective-permute-done((bf16[256,2048]{1,0:T(8,128)(2,1)S(1)}, bf16[256,2048]{1,0:T(8,128)(2,1)S(1)}, u32[]{:S(2)}, u32[]{:S(2)}) %collective-permute-start.5) | collective-permute-done | bytes 1048608 | tf_op jit(solution)/shard_map/ppermute | solution.py:14
  800.6 33.1 %collective-permute-done.6 = bf16[256,2048]{1,0:T(8,128)(2,1)} collective-permute-done((bf16[256,2048]{1,0:T(8,128)(2,1)S(1)}, bf16[256,2048]{1,0:T(8,128)(2,1)}, u32[]{:S(2)}, u32[]{:S(2)}) %collective-permute-start.6) | collective-permute-done | bytes 1048608 | tf_op jit(solution)/shard_map/ppermute | solution.py:14
  833.7 5.9 collective-permute-start.7
  839.6 145.5 %reduce-scatter.3.cloned.1.call-done = f32[128,2048]{0,1:T(8,128)} async-done(((f32[2048,2048]{0,1:T(8,128)}), f32[128,2048]{0,1:T(8,128)}) %reduce-scatter.3.cloned.1.call-update) | async-done | bytes 1048592 | tf_op jit(solution)/shard_map/reduce_scatter | solution.py:151
  987.0 11.5 %rev.10 = bf16[256,2048]{1,0:T(8,128)(2,1)} reverse(bf16[256,2048]{1,0:T(8,128)(2,1)S(1)} %collective-permute-done.7), dimensions={0,1} | reverse | bytes 2097152 | tf_op jit(solution)/shard_map/rev | solution.py:129
  1001.2 78.3 %all-reduce.17.cloned.1.call-done = (f32[128,2048]{0,1:T(8,128)}, f32[128,160]{0,1:T(8,128)}) async-done(((f32[128,2048]{0,1:T(8,128)}, f32[128,160]{0,1:T(8,128)}), (f32[128,2048]{0,1:T(8,128)}, f32[128,160]{0,1:T(8,128)})) %all-reduce.17.cloned.1.call-update) | async-done | bytes 1130512 | tf_op jit(solution)/shard_map/psum | solution.py:154
  (394 shorter events, 252.8 us)
Async XLA Ops:
  7.2 128.4 %copy-start = (bf16[2048,160]{0,1:T(8,128)(2,1)S(1)}, bf16[2048,160]{0,1:T(8,128)(2,1)}, u32[]{:S(2)}) copy-start(bf16[2048,160]{0,1:T(8,128)(2,1)} %param.14) | copy-start | bytes 1966084
  7.2 16.5 %copy-start.22 = (bf16[1,256,2048]{2,1,0:T(8,128)(2,1)S(1)}, bf16[1,256,2048]{2,1,0:T(8,128)(2,1)}, u32[]{:S(2)}) copy-start(bf16[1,256,2048]{2,1,0:T(8,128)(2,1)} %param.18) | copy-start | bytes 3145732
  7.2 267.0 %all-gather.11.cloned.1.call-start = ((), (), s32[]{:S(2)}) async-start(), calls=%async_computation.4 | async-start | bytes 17825792 | tf_op jit(solution)/shard_map/all_gather | solution.py:19
  23.7 103.7 %copy-start.11 = (bf16[1,256,2048]{2,1,0:T(8,128)(2,1)S(1)}, bf16[1,256,2048]{2,1,0:T(8,128)(2,1)}, u32[]{:S(2)}) copy-start(bf16[1,256,2048]{2,1,0:T(8,128)(2,1)} %param.12) | copy-start | bytes 3145732
  25.2 4.2 collective-permute-start
  29.4 47.7 %collective-permute-start.1 = (bf16[2,256,2048]{2,1,0:T(8,128)(2,1)S(1)}, bf16[2,256,2048]{2,1,0:T(8,128)(2,1)S(1)}, u32[]{:S(2)}, u32[]{:S(2)}) collective-permute-start(bf16[2,256,2048]{2,1,0:T(8,128)(2,1)S(1)} %collective-permute-done), channel_id=1, source_target_pairs={{0,2},{1,3},{2,0},{3,1},{4,6},{5,7},{6,4},{7,5},{8,10},{9,11},{10,... | collective-permute-start | bytes 6291464 | tf_op jit(solution)/shard_map/ppermute | solution.py:14
  77.1 46.9 %collective-permute-start.2 = (bf16[2,256,2048]{2,1,0:T(8,128)(2,1)S(1)}, bf16[2,256,2048]{2,1,0:T(8,128)(2,1)}, u32[]{:S(2)}, u32[]{:S(2)}) collective-permute-start(bf16[2,256,2048]{2,1,0:T(8,128)(2,1)S(1)} %collective-permute-done.1), channel_id=1, source_target_pairs={{0,4},{1,5},{2,6},{3,7},{4,0},{5,1},{6,2},{7,3},{8,12},{9,13},{10,... | collective-permute-start | bytes 6291464 | tf_op jit(solution)/shard_map/ppermute | solution.py:14
  124.1 47.8 %collective-permute-start.3 = (bf16[2,256,2048]{2,1,0:T(8,128)(2,1)}, bf16[2,256,2048]{2,1,0:T(8,128)(2,1)}, u32[]{:S(2)}, u32[]{:S(2)}) collective-permute-start(bf16[2,256,2048]{2,1,0:T(8,128)(2,1)} %collective-permute-done.2), channel_id=1, source_target_pairs={{0,8},{1,9},{2,10},{3,11},{4,12},{5,13},{6,14},{7,15},{8,0},{9,1},... | collective-permute-start | bytes 6291464 | tf_op jit(solution)/shard_map/ppermute | solution.py:14
  135.5 296.6 %copy-start.8 = (bf16[256,2048]{0,1:T(8,128)(2,1)}, bf16[256,2048]{0,1:T(8,128)(2,1)S(1)}, u32[]{:S(2)}) copy-start(bf16[256,2048]{0,1:T(8,128)(2,1)S(1)} %copy.66) | copy-start | bytes 3145732
  135.6 38.0 %copy-start.77 = (f32[32]{0:T(128)S(1)}, f32[32]{0:T(128)}, u32[]{:S(2)}) copy-start(f32[32]{0:T(128)} %param.16) | copy-start | bytes 388
  135.6 38.7 %copy-start.88 = (f32[32]{0:T(128)}, f32[32]{0:T(128)S(1)}, u32[]{:S(2)}) copy-start(f32[32]{0:T(128)S(1)} %exponential_negate_fusion) | copy-start | bytes 388
  176.5 10.4 copy-start.81
  180.0 189.1 %all-gather.13.cloned.1.call-start = ((), (), s32[]{:S(2)}) async-start(), calls=%async_computation.5 | async-start | bytes 17825792 | tf_op jit(solution)/shard_map/all_gather | solution.py:19
  193.1 343.6 %all-gather.15.cloned.1.call-start = ((), (), s32[]{:S(2)}) async-start(), calls=%async_computation.6 | async-start | bytes 17825792 | tf_op jit(solution)/shard_map/all_gather | solution.py:19
  444.0 186.9 %all-gather.17.cloned.1.call-start = ((), (), s32[]{:S(2)}) async-start(), calls=%async_computation.7 | async-start | bytes 17825792 | tf_op jit(solution)/shard_map/all_gather | solution.py:19
  461.1 10.2 copy-start.46
  486.7 352.9 %reduce-scatter.5.cloned.1.call-start = ((), (), s32[]{:S(2)}) async-start(), calls=%async_computation.3 | async-start | bytes 1392640 | tf_op jit(solution)/shard_map/reduce_scatter | solution.py:152
  492.6 14.3 %copy-start.51 = (f32[256,32]{0,1:T(8,128)S(1)}, f32[256,32]{0,1:T(8,128)}, u32[]{:S(2)}) copy-start(f32[256,32]{0,1:T(8,128)} %get-tuple-element.471) | copy-start | bytes 98308
  715.1 10.1 copy-start.37
  722.6 9.8 copy-start.41
  722.6 9.8 copy-start.42
  722.6 9.9 copy-start.49
  735.7 249.4 %reduce-scatter.3.cloned.1.call-start = ((), (), s32[]{:S(2)}) async-start(), calls=%async_computation.2 | async-start | bytes 17825792 | tf_op jit(solution)/shard_map/reduce_scatter | solution.py:151
  764.6 220.6 %copy-start.18 = (f32[256,32,64]{0,2,1:T(8,128)S(1)}, f32[256,32,64]{0,2,1:T(8,128)}, u32[]{:S(2)}) copy-start(f32[256,32,64]{0,2,1:T(8,128)} %copy-done.17) | copy-start | bytes 6291460
  764.6 314.8 %all-reduce.17.cloned.1.call-start = ((), (), s32[]{:S(2)}) async-start(), calls=%async_computation.8 | async-start | bytes 2260992 | tf_op jit(solution)/shard_map/psum | solution.py:154
  765.8 2.7 collective-permute-start.4
  768.5 31.3 %collective-permute-start.5 = (bf16[256,2048]{1,0:T(8,128)(2,1)S(1)}, bf16[256,2048]{1,0:T(8,128)(2,1)S(1)}, u32[]{:S(2)}, u32[]{:S(2)}) collective-permute-start(bf16[256,2048]{1,0:T(8,128)(2,1)S(1)} %collective-permute-done.4), channel_id=1, source_target_pairs={{0,2},{1,3},{2,0},{3,1},{4,6},{5,7},{6,4},{7,5},{8,10},{9,11},{10,... | collective-permute-start | bytes 3145736 | tf_op jit(solution)/shard_map/ppermute | solution.py:14
  799.8 34.0 %collective-permute-start.6 = (bf16[256,2048]{1,0:T(8,128)(2,1)S(1)}, bf16[256,2048]{1,0:T(8,128)(2,1)}, u32[]{:S(2)}, u32[]{:S(2)}) collective-permute-start(bf16[256,2048]{1,0:T(8,128)(2,1)S(1)} %collective-permute-done.5), channel_id=1, source_target_pairs={{0,4},{1,5},{2,6},{3,7},{4,0},{5,1},{6,2},{7,3},{8,12},{9,13},{10,... | collective-permute-start | bytes 3145736 | tf_op jit(solution)/shard_map/ppermute | solution.py:14
  833.7 153.3 %collective-permute-start.7 = (bf16[256,2048]{1,0:T(8,128)(2,1)}, bf16[256,2048]{1,0:T(8,128)(2,1)S(1)}, u32[]{:S(2)}, u32[]{:S(2)}) collective-permute-start(bf16[256,2048]{1,0:T(8,128)(2,1)} %collective-permute-done.6), channel_id=1, source_target_pairs={{0,8},{1,9},{2,10},{3,11},{4,12},{5,13},{6,14},{7,15},{8,0},{9,1},... | collective-permute-start | bytes 3145736 | tf_op jit(solution)/shard_map/ppermute | solution.py:14
  985.2 13.3 %copy-start.80 = (f32[256]{0:T(256)S(1)}, f32[256]{0:T(256)}, u32[]{:S(2)}) copy-start(f32[256]{0:T(256)} %copy-done.79) | copy-start | bytes 3076
  987.0 11.5 %copy-start.20 = (f32[256,2048]{1,0:T(8,128)S(1)}, f32[256,2048]{1,0:T(8,128)}, u32[]{:S(2)}) copy-start(f32[256,2048]{1,0:T(8,128)} %copy.72) | copy-start | bytes 6291460
  998.5 84.1 %copy-start.1 = (bf16[2048,160]{0,1:T(8,128)(2,1)S(1)}, bf16[2048,160]{0,1:T(8,128)(2,1)}, u32[]{:S(2)}) copy-start(bf16[2048,160]{0,1:T(8,128)(2,1)} %param.14) | copy-start | bytes 1966084
  (75 other events, 330.0 us)
Sparse Core Ops, SparseCore 0:
  180.1 94.0 all-gather.10
  276.4 92.5 all-gather.12
  444.1 92.5 all-gather.14
  538.3 92.5 all-gather.16
  735.9 66.0 reduce-scatter.4
  804.2 180.9 reduce-scatter.2
  987.7 91.6 all-reduce.16
where the time goes:
time: 1100 us; the launch traced here: 1090 us
  waiting for transfers between devices  640 us (58%)
  local copies, waits for them, and re-layouts  133 us (12%)
  matrix products  121 us (11%)
  other arithmetic  118 us (11%)
  blocking collectives  45.8 us (4%)
  between operations  15.8 us (1%)
  starting transfers between devices  15.6 us (1%)
    all_gather x4, waiting for transfers between devices, carried_in(): everything = jax.tree.map(lambda part: lax.all_gather(part, axis), array)  220 us
    ppermute x8, waiting for transfers between devices, swapped(): lax.ppermute(array, axis, [(i, i ^ 1 << apart) for i in range(lax.axis_si...  197 us
    reduce_scatter x1, waiting for transfers between devices, shards(): lax.psum_scatter(term_x, 'ctx', scatter_dimension=0, tiled=True)  146 us
    select_n x32, other arithmetic, step(): return jax.tree.map(lambda a, b: jnp.where(reached, a, b), new, before)  79.8 us
    psum x1, waiting for transfers between devices, shards(): grad_x, grad_small = lax.psum((shard_x, shard_small), 'dp')  78.3 us
    mul x64, local copies, waits for them, and re-layouts, chain(): later[0][:, None, None] * earlier[1] + later[1]  60.6 us
    dot_general x6, matrix products, forward_y(): inner = jnp.einsum('hts,shp->thp', mixing, per_head, precision=precise)  51.3 us
    all_gather x2, blocking collectives, carried_in(): everything = jax.tree.map(lambda part: lax.all_gather(part, axis), array)  45.8 us
  transfers between devices with their start and end apart: 15, of which 13 were waited for; matrix products, arithmetic and copies ran while one was open for 15% of the time, Pallas kernels for 0%

commit v1 on v0

v1 whole, which is shorter than its diff:
```python
import jax
import jax.numpy as jnp
from jax import lax
from jax.experimental import pallas as pl
from jax.experimental.pallas import tpu as pltpu
from jax.sharding import PartitionSpec as P

HEAD = 64
STATE = 64
D = 2048
ROWS = 256
T2 = 2 * ROWS
HEADS = 32
PAIRS = 16
PEERS = 16
SLOT = 144
WIDE = 2304
PARTS = 3
COLS = WIDE // PARTS
MESH = pl.DeviceIdType.MESH
BF = jnp.bfloat16
F32 = jnp.float32
LOG2E = 1.4426950408889634

NN = (((1,), (0,)), ((), ()))
NT = (((1,), (1,)), ((), ()))
TN = (((0,), (0,)), ((), ()))


def dot(a, b, dims=NN):
    return lax.dot_general(a, b, dims, preferred_element_type=F32)


def dot_exact(a, b, dims=NN):
    return lax.dot_general(
        a, b, dims, preferred_element_type=F32, precision=lax.Precision.HIGHEST
    )


def iota2(shape, dim):
    return lax.broadcasted_iota(jnp.int32, shape, dim)


def flip_matrix(n):
    return (iota2((n, n), 0) + iota2((n, n), 1) == n - 1).astype(F32).astype(BF)


def project_kernel(rows_ref, wx_ref, ws_ref, rt_ref, xt_ref, proj_ref, r_ref):
    step = pl.program_id(0)

    @pl.when(step == 0)
    def _():
        flip = flip_matrix(256)
        for blk in range(8):
            part = rows_ref[:, blk * 256 : (blk + 1) * 256]
            r_ref[0:ROWS, blk * 256 : (blk + 1) * 256] = part
            r_ref[ROWS:T2, (7 - blk) * 256 : (8 - blk) * 256] = dot(part, flip).astype(BF)
            across = part.T
            rt_ref[blk * 256 : (blk + 1) * 256, 0:ROWS] = across
            rt_ref[(7 - blk) * 256 : (8 - blk) * 256, ROWS:T2] = dot(flip, across).astype(BF)
        proj_ref[...] = jnp.zeros_like(proj_ref)
        proj_ref[:, 0:160] = dot(r_ref[...], ws_ref[...])

    xt_ref[...] = dot(r_ref[...], wx_ref[...]).astype(BF).T


def project(rows, x_weight, state_weight):
    cols = 256
    return pl.pallas_call(
        project_kernel,
        grid=(D // cols,),
        in_specs=[
            pl.BlockSpec((ROWS, D), lambda i: (0, 0)),
            pl.BlockSpec((D, cols), lambda i: (0, i)),
            pl.BlockSpec((D, 160), lambda i: (0, 0)),
        ],
        out_specs=[
            pl.BlockSpec((D, T2), lambda i: (0, 0)),
            pl.BlockSpec((cols, T2), lambda i: (i, 0)),
            pl.BlockSpec((T2, 256), lambda i: (0, 0)),
        ],
        out_shape=[
            jax.ShapeDtypeStruct((D, T2), BF),
            jax.ShapeDtypeStruct((D, T2), BF),
            jax.ShapeDtypeStruct((T2, 256), F32),
        ],
        scratch_shapes=[pltpu.VMEM((T2, D), BF)],
        compiler_params=pltpu.CompilerParams(vmem_limit_bytes=48 * 2**20),
        name="project",
    )(rows, x_weight, state_weight)


def scan_kernel(
    xt_ref, proj_ref, cot_ref, gain_ref, lr_ref, sb_ref,
    mixed_ref, dxt_ref,
    small, zt, step_t, weight, l2_t, l2_n, el_t, bdb, bdbt, bdc, bdct, scm, dsc,
    wx, ct, u, g, du, vdu, mst, dec, tot, prow, qrow, q2row, asrow,
    send_a, recv_a, send_a2, recv_a2, send_b, recv_b, send_b2, recv_b2, up,
    sa, ra, sa2, ra2, sb, rb, sb2, rb2,
):
    me = lax.axis_index("ctx")
    barrier = pltpu.get_barrier_semaphore()

    def greet(j, c):
        @pl.when(j != me)
        def _():
            pl.semaphore_signal(barrier, inc=1, device_id={"ctx": j}, device_id_type=MESH)
        return c

    lax.fori_loop(0, PEERS, greet, 0)

    def copy(src, dst, ssem, rsem, to, slot):
        return pltpu.make_async_remote_copy(
            src_ref=src.at[to], dst_ref=dst.at[slot], send_sem=ssem.at[to],
            recv_sem=rsem.at[slot], device_id={"ctx": to}, device_id_type=MESH,
        )

    def send_all(src, dst, ssem, rsem):
        def one(k, c):
            j = lax.rem(me + k, PEERS)
            copy(src, dst, ssem, rsem, j, me).start()
            return c
        lax.fori_loop(1, PEERS, one, 0)

    def recv_all(src, dst, ssem, rsem):
        def one(k, c):
            j = lax.rem(me + k, PEERS)
            copy(src, dst, ssem, rsem, j, j).wait_recv()
            return c
        lax.fori_loop(1, PEERS, one, 0)

    def sent_all(src, dst, ssem, rsem):
        def one(k, c):
            j = lax.rem(me + k, PEERS)
            copy(src, dst, ssem, rsem, j, me).wait_send()
            return c
        lax.fori_loop(1, PEERS, one, 0)

    low = iota2((1, 128), 1) < 64
    row_i = iota2((ROWS, ROWS), 0)
    col_i = iota2((ROWS, ROWS), 1)
    causal = (row_i >= col_i, row_i <= col_i)
    tri = [m.astype(F32) for m in causal]
    halves = (slice(0, ROWS), slice(ROWS, T2))

    small[...] = jnp.zeros_like(small)
    small[0:1, 0:HEADS] = -jnp.exp(lr_ref[...])
    small[1:2, 0:HEADS] = sb_ref[...]
    neg_rate = small[0:1, :]
    z = proj_ref[:, 128:256] + small[1:2, :]
    step_n = jnp.maximum(z, 0.0) + jnp.log1p(jnp.exp(-jnp.abs(z)))
    log_n = step_n * (neg_rate * LOG2E)
    zt[...] = z.T[0:HEADS]
    step_t[...] = step_n.T[0:HEADS]
    for b in range(2):
        l2 = dot_exact(tri[b], log_n[halves[b]])
        l2_n[b] = l2
        l2_t[:, halves[b]] = l2.T[0:HEADS]
    el_t[...] = jnp.exp2(l2_t[...])
    ends = (l2_t[:, ROWS - 1 : ROWS], l2_t[:, ROWS : ROWS + 1])
    tot[...] = jnp.exp2(jnp.where(low, ends[0], ends[1]))
    for b in range(2):
        weight[:, halves[b]] = step_t[:, halves[b]] * jnp.exp2(ends[b] - l2_t[:, halves[b]])

    both = proj_ref[:, 0:128]
    turned = pltpu.roll(both, 64, 1)
    own = (iota2((T2, 128), 0) < ROWS) == (iota2((T2, 128), 1) < 64)
    maps_b = jnp.where(low, both, turned)
    maps_c = jnp.where(low, turned, both)
    b_diag = jnp.where(own, maps_b, 0.0)
    c_diag = jnp.where(own, maps_c, 0.0)
    for full, by_rows, by_cols in ((b_diag, bdb, bdbt), (c_diag, bdc, bdct)):
        coarse = full.astype(BF).astype(F32)
        for k, term in enumerate((coarse, full - coarse)):
            by_rows[:, k * 128 : (k + 1) * 128] = term.astype(BF)
            by_cols[k * 128 : (k + 1) * 128, :] = term.T.astype(BF)

    def to_state(lhs, by_rows):
        out = dot(lhs, by_rows[...])
        return (out[:, 0:128] + out[:, 128:256]).astype(BF)

    def from_state(state, by_cols):
        return dot(jnp.concatenate([state, state], axis=1), by_cols[...])

    def local_end(hp, c):
        base = pl.multiple_of(hp * 128, 128)
        for hh in range(2):
            rows = pl.ds(pl.multiple_of(base + hh * 64, 64), 64)
            h = pl.ds(2 * hp + hh, 1)
            wx[rows, :] = (xt_ref[rows, :].astype(F32) * weight[h, :]).astype(BF)
        send_a[hp, 0:128, :] = to_state(wx[pl.ds(base, 128), :], bdb)
        t0 = tot[pl.ds(2 * hp, 1), :]
        t1 = tot[pl.ds(2 * hp + 1, 1), :]
        h0 = t0.astype(BF).astype(F32)
        h1 = t1.astype(BF).astype(F32)
        at = iota2((16, 128), 0)
        extra = jnp.where(at == 0, h0, jnp.where(at == 1, t0 - h0, jnp.where(at == 2, h1, t1 - h1)))
        send_a[hp, 128:144, :] = extra.astype(BF)
        return c

    lax.fori_loop(0, PAIRS, local_end, 0)
    recv_a[me] = send_a[me]
    pl.semaphore_wait(barrier, PEERS - 1)
    send_all(send_a, recv_a, sa, ra)

    for b in range(2):
        sc = dot_exact(
            jnp.where(low, maps_c[halves[b]], 0.0), maps_b[halves[b]], NT
        )
        scm[b] = jnp.where(causal[b], sc, 0.0)

    zero_half = jnp.zeros((128, 128), BF)
    blocks = (((0, 0), (1, 0), (1, 1)), ((0, 0), (0, 1), (1, 1)))

    def span(i):
        return slice(i * 128, (i + 1) * 128)

    def forward(hp, c):
        for hh in range(2):
            h = 2 * hp + hh
            rows = pl.ds(pl.multiple_of(h * 64, 64), 64)
            for b in range(2):
                column = pltpu.roll(l2_n[b], 128 - h, 1)[:, 0:1]
                line = l2_t[pl.ds(h, 1), halves[b]]
                size = step_t[pl.ds(h, 1), halves[b]]
                for i, j in blocks[b]:
                    d = jnp.exp2(jnp.minimum(column[span(i)] - line[:, span(j)], 0.0))
                    d = d * size[:, span(j)]
                    dec[b, h, span(i), span(j)] = d.astype(BF)
                    mst[b, h, span(i), span(j)] = (d * scm[b, span(i), span(j)]).astype(BF)
                mst[b, h, span(b), span(1 - b)] = zero_half
                u[rows, halves[b]] = dot(xt_ref[rows, halves[b]], mst[b, h], NT)
        return c

    def chain(recv, out, fwd_up):
        def totals(i):
            t = recv_a[i, 128:144, :].astype(F32)
            rows = iota2((128, 128), 0) < 64
            return jnp.where(rows, t[0:1] + t[1:2], t[2:3] + t[3:4])

        def climb(i, carry):
            up[i] = carry
            return totals(i) * carry + recv[i, 0:128, :].astype(F32)

        zero = jnp.zeros((128, 128), F32)
        lax.fori_loop(0, PEERS, climb, zero)

        def descend(k, carry):
            i = PEERS - 1 - k
            pick = low if fwd_up else jnp.logical_not(low)
            out[i] = jnp.where(pick, up[i], carry).astype(BF)
            return totals(i) * carry + recv[i, 0:128, :].astype(F32)

        lax.fori_loop(0, PEERS, descend, zero)

    lax.fori_loop(0, PAIRS // 2, forward, 0)
    recv_all(send_a, recv_a, sa, ra)
    chain(recv_a, send_a2, True)
    recv_a2[me] = send_a2[me]
    send_all(send_a2, recv_a2, sa2, ra2)
    lax.fori_loop(PAIRS // 2, PAIRS, forward, 0)

    flip = flip_matrix(256)
    for blk in range(8):
        turned_c = cot_ref[:, blk * 256 : (blk + 1) * 256].T
        ct[blk * 256 : (blk + 1) * 256, 0:ROWS] = turned_c
        ct[(7 - blk) * 256 : (8 - blk) * 256, ROWS:T2] = dot(flip, turned_c).astype(BF)

    recv_all(send_a2, recv_a2, sa2, ra2)

    def gains(hp):
        lane = pl.ds(pl.multiple_of(hp * 128, 128), 128)
        column = jnp.broadcast_to(gain_ref[:, lane], (128, 128)).T
        return jnp.concatenate([column] * 4, axis=1)

    def readout(hp, c):
        q, e = c
        base = pl.multiple_of(hp * 128, 128)
        out = from_state(recv_a2[hp], bdct)
        gain = gains(hp)
        for hh in range(2):
            rows = pl.ds(pl.multiple_of(base + hh * 64, 64), 64)
            part = slice(hh * 64, hh * 64 + 64)
            v = u[rows, :] + out[part] * el_t[pl.ds(2 * hp + hh, 1), :]
            u[rows, :] = v
            q = q + jnp.sum(v * v, axis=0, keepdims=True)
            e = e + jnp.sum(v * gain[part] * ct[rows, :].astype(F32), axis=0, keepdims=True)
        return q, e

    none = jnp.zeros((1, T2), F32)
    q, e = lax.fori_loop(0, PAIRS, readout, (none, none))
    scale = lax.rsqrt(q * (1.0 / D) + 1e-05)
    pull = scale * scale * scale * e * (1.0 / D)

    def normed(hp, c):
        base = pl.multiple_of(hp * 128, 128)
        gain = gains(hp)
        for hh in range(2):
            rows = pl.ds(pl.multiple_of(base + hh * 64, 64), 64)
            h = pl.ds(2 * hp + hh, 1)
            part = slice(hh * 64, hh * 64 + 64)
            v = u[rows, :]
            gs = gain[part] * scale
            back = gs * ct[rows, :].astype(F32) - v * pull
            vdu[rows, :] = (back * el_t[h, :]).astype(BF)
            back = back.astype(BF)
            du[rows, :] = back
            prow[h, :] = jnp.sum(back.astype(F32) * v, axis=0, keepdims=True)
            u[rows, :] = v * gs
        send_b[hp] = to_state(vdu[pl.ds(base, 128), :], bdc)
        return c

    lax.fori_loop(0, PAIRS, normed, 0)
    recv_b[me] = send_b[me]
    send_all(send_b, recv_b, sb, rb)
    dsc[...] = jnp.zeros_like(dsc)

    def backward(hp, c):
        for b in range(2):
            pair = []
            for hh in range(2):
                h = 2 * hp + hh
                rows = pl.ds(pl.multiple_of(h * 64, 64), 64)
                d = du[rows, halves[b]]
                g[rows, halves[b]] = dot(d, mst[b, h])
                pair.append(dot(d, xt_ref[rows, halves[b]], TN))
            for i, j in blocks[b]:
                acc = dsc[b, span(i), span(j)]
                for hh in range(2):
                    acc = acc + pair[hh][span(i), span(j)] * dec[
                        b, 2 * hp + hh, span(i), span(j)
                    ].astype(F32)
                dsc[b, span(i), span(j)] = acc
        return c

    lax.fori_loop(0, PAIRS // 2, backward, 0)
    recv_all(send_b, recv_b, sb, rb)
    chain(recv_b, send_b2, False)
    recv_b2[me] = send_b2[me]
    send_all(send_b2, recv_b2, sb2, rb2)
    lax.fori_loop(PAIRS // 2, PAIRS, backward, 0)

    for blk in range(8):
        y_rc = u[(7 - blk) * 256 : (8 - blk) * 256, ROWS:T2].astype(BF)
        y = u[blk * 256 : (blk + 1) * 256, 0:ROWS] + dot(flip, y_rc)
        mixed_ref[:, blk * 256 : (blk + 1) * 256] = y.astype(BF).T

    def read_maps(hp, acc):
        return acc + dot(recv_a2[hp], vdu[pl.ds(pl.multiple_of(hp * 128, 128), 128), :], TN)

    dc_state = lax.fori_loop(0, PAIRS, read_maps, jnp.zeros((128, T2), F32))

    recv_all(send_b2, recv_b2, sb2, rb2)

    def finish(hp, acc):
        base = pl.multiple_of(hp * 128, 128)
        after = recv_b2[hp]
        acc = acc + dot(after, wx[pl.ds(base, 128), :], TN)
        out = from_state(after, bdbt)
        meet = after.astype(F32) * recv_a2[hp].astype(F32)
        for hh in range(2):
            rows = pl.ds(pl.multiple_of(base + hh * 64, 64), 64)
            h = pl.ds(2 * hp + hh, 1)
            part = slice(hh * 64, hh * 64 + 64)
            asrow[h, :] = jnp.sum(meet[part], axis=0, keepdims=True)
            far = out[part] * weight[h, :]
            whole = g[rows, :] + far
            dxt_ref[rows, :] = whole.astype(BF)
            x = xt_ref[rows, :].astype(F32)
            qrow[h, :] = jnp.sum(x * whole, axis=0, keepdims=True)
            q2row[h, :] = jnp.sum(x * far, axis=0, keepdims=True)
        return acc

    db_state = lax.fori_loop(0, PAIRS, finish, jnp.zeros((128, T2), F32))

    met = asrow[...] * tot[...]
    neg_col = jnp.broadcast_to(neg_rate, (128, 128)).T[0:HEADS, 0:1]
    for b in range(2):
        lanes = halves[b]
        mine = low if b == 0 else jnp.logical_not(low)
        end_grad = jnp.sum(jnp.where(mine, met, 0.0), axis=1, keepdims=True) + jnp.sum(
            q2row[:, lanes], axis=1, keepdims=True
        )
        dl = prow[:, lanes] - qrow[:, lanes]
        da = dot_exact(dl, tri[b]) + end_grad
        zb = zt[:, lanes]
        small_e = jnp.exp(-jnp.abs(zb))
        sig = jnp.where(zb >= 0, 1.0, small_e) / (1.0 + small_e)
        ratio = jnp.where(zb < -20.0, 1.0, sig / step_t[:, lanes])
        dz = qrow[:, lanes] * ratio + da * neg_col * sig
        dxt_ref[D + 128 : D + 160, lanes] = dz.astype(BF)
        d_scores = jnp.where(causal[b], dsc[b], 0.0).astype(BF)
        part = slice(b * 64, b * 64 + 64)
        dc = dot(bdbt[part, lanes], d_scores, NT) + dc_state[part, lanes]
        db = dot(bdct[part, lanes], d_scores) + db_state[part, lanes]
        dxt_ref[D : D + 64, lanes] = db.astype(BF)
        dxt_ref[D + 64 : D + 128, lanes] = dc.astype(BF)

    dxt_ref[D + 160 : WIDE, :] = jnp.zeros((WIDE - D - 160, T2), BF)
    sent_all(send_a, recv_a, sa, ra)
    sent_all(send_a2, recv_a2, sa2, ra2)
    sent_all(send_b, recv_b, sb, rb)
    sent_all(send_b2, recv_b2, sb2, rb2)


def scan(xt, proj, cot, gain, log_rates, step_bias):
    vmem = pl.BlockSpec(memory_space=pltpu.VMEM)
    V = pltpu.VMEM
    slots = [V((PEERS, SLOT, 128), BF)] * 2 + [V((PEERS, 128, 128), BF)] * 6
    return pl.pallas_call(
        scan_kernel,
        in_specs=[vmem] * 6,
        out_specs=[vmem] * 2,
        out_shape=[
            jax.ShapeDtypeStruct((ROWS, D), BF),
            jax.ShapeDtypeStruct((WIDE, T2), BF),
        ],
        scratch_shapes=[
            V((8, 128), F32),
            V((HEADS, T2), F32),
            V((HEADS, T2), F32),
            V((HEADS, T2), F32),
            V((HEADS, T2), F32),
            V((2, ROWS, 128), F32),
            V((HEADS, T2), F32),
            V((T2, 256), BF),
            V((256, T2), BF),
            V((T2, 256), BF),
            V((256, T2), BF),
            V((2, ROWS, ROWS), F32),
            V((2, ROWS, ROWS), F32),
            V((D, T2), BF),
            V((D, T2), BF),
            V((D, T2), F32),
            V((D, T2), F32),
            V((D, T2), BF),
            V((D, T2), BF),
            V((2, HEADS, ROWS, ROWS), BF),
            V((2, HEADS, ROWS, ROWS), BF),
            V((HEADS, 128), F32),
            V((HEADS, T2), F32),
            V((HEADS, T2), F32),
            V((HEADS, T2), F32),
            V((HEADS, 128), F32),
        ]
        + slots
        + [V((PEERS, 128, 128), F32)]
        + [pltpu.SemaphoreType.DMA((PEERS,))] * 8,
        compiler_params=pltpu.CompilerParams(
            collective_id=0, has_side_effects=True, vmem_limit_bytes=60 * 2**20
        ),
        name="scan",
    )(xt, proj, cot, gain, log_rates, step_bias)


def grads_kernel(
    rt_ref, dx_ref, gx_ref, gs_ref,
    rt_in, dx_in, acc, buf1, in1, buf2, in2, buf3, in3, last, out_in,
    core_s, core_r, ss, rs, out_s, out_r,
):
    dp = lax.axis_index("dp")
    ctx = lax.axis_index("ctx")
    zz, x_hi = dp // 2, dp % 2
    yy, x_lo, core = ctx // 4, (ctx // 2) % 2, ctx % 2
    xx = x_hi * 2 + x_lo
    coords = {"z": zz, "y": yy, "x": xx}

    def at(axis, v):
        if axis == "z":
            return {"dp": v * 2 + x_hi, "ctx": ctx}
        if axis == "y":
            return {"dp": dp, "ctx": (v * 2 + x_lo) * 2 + core}
        return {"dp": zz * 2 + v // 2, "ctx": (yy * 2 + v % 2) * 2 + core}

    sibling = {"dp": dp, "ctx": yy * 4 + x_lo * 2 + (1 - core)}
    barrier = pltpu.get_barrier_semaphore()
    friends = [sibling]
    friends += [{"dp": (dp + k) % 8, "ctx": ctx} for k in range(1, 8)]
    friends += [at("y", (yy + k) % 4) for k in range(1, 4)]
    friends += [at("x", (xx + k) % 4) for k in (1, 3)]
    for friend in friends:
        pl.semaphore_signal(barrier, inc=1, device_id=friend, device_id_type=MESH)
    pl.semaphore_wait(barrier, len(friends))

    def to(friend, src, dst, ssem, rsem):
        return pltpu.make_async_remote_copy(
            src_ref=src, dst_ref=dst, send_sem=ssem, recv_sem=rsem,
            device_id=friend, device_id_type=MESH,
        )

    swaps = [to(sibling, rt_ref.at[:, 1 - core], rt_in, core_s.at[3], core_r.at[3])]
    swaps += [
        to(sibling, dx_ref.at[p], dx_in.at[p], core_s.at[p], core_r.at[p])
        for p in range(PARTS)
    ]
    for swap in swaps:
        swap.start()

    for p in range(PARTS):
        def own(jj, c, p=p):
            acc[p, jj] = dot(rt_ref[jj, core], dx_ref[p], NT)
            return c
        lax.fori_loop(0, 8, own, 0)

    orders = (("z", "y", "x"), ("y", "x", "z"), ("x", "z", "y"))
    stages = ((buf1, in1), (buf2, in2), (buf3, in3))

    def moves(p, stage):
        axis = orders[p][stage]
        here = coords[axis]
        buf, into = stages[stage]
        found = []
        for k in (2, 1, 3):
            v = (here + k) % 4

            def copy(slot, v=v):
                return to(
                    at(axis, v), buf.at[p, v], into.at[p, slot],
                    ss.at[p, stage, v], rs.at[p, stage, slot],
                )

            found.append((v, lambda copy=copy: copy(here), lambda copy=copy, v=v: copy(v)))
        return found

    def launch(p, stage):
        for v, out, back in moves(p, stage):
            out().start()

    def collect(p, stage):
        buf, into = stages[stage]
        found = moves(p, stage)
        for v, out, back in found:
            back().wait_recv()
        total = buf[p, coords[orders[p][stage]]].astype(F32)
        for v, out, back in found:
            total = total + into[p, v].astype(F32)
        return total

    swaps[0].wait_recv()
    for p in range(PARTS):
        swaps[1 + p].wait_recv()

        def both(jj, c, p=p):
            tile = (acc[p, jj] + dot(rt_in[jj], dx_in[p], NT)).astype(BF)
            y_to, x_lo_to = jj // 2, jj % 2
            for k in range(8):
                where = {"z": k // 2, "y": y_to, "x": (k % 2) * 2 + x_lo_to}
                a, b, d = (where[axis] for axis in orders[p])
                buf1[p, a, b, d] = tile[k * 16 : (k + 1) * 16]
            return c
        lax.fori_loop(0, 8, both, 0)
        launch(p, 0)

    for p in range(PARTS):
        found = moves(p, 0)
        for v, out, back in found:
            back().wait_recv()
        here = coords[orders[p][0]]

        def add(i, c, p=p, here=here, found=found):
            total = buf1[p, here, i].astype(F32)
            for v, out, back in found:
                total = total + in1[p, v, i].astype(F32)
            buf2[p, i] = total.astype(BF)
            return c
        lax.fori_loop(0, 4, add, 0)
        launch(p, 1)
    for p in range(PARTS):
        buf3[p] = collect(p, 1)
        launch(p, 2)
    for p in range(PARTS):
        last[:, p * COLS : (p + 1) * COLS] = collect(p, 2).astype(BF)

    shares = []
    for k in range(1, 8):
        j = (dp + k) % 8
        friend = {"dp": j, "ctx": ctx}
        out = to(friend, last, out_in.at[dp], out_s.at[j], out_r.at[dp])
        back = to(friend, last, out_in.at[j], out_s.at[j], out_r.at[j])
        out.start()
        shares.append((j, out, back))
    out_in[dp] = last[...]
    for j, out, back in shares:
        back.wait_recv()
    for k in range(8):
        piece = out_in[k].astype(F32)
        gx_ref[k * 16 : (k + 1) * 16, :] = piece[:, 0:D]
        gs_ref[k * 16 : (k + 1) * 16, :] = piece[:, D : D + 160]

    for swap in swaps:
        swap.wait_send()
    for p in range(PARTS):
        for stage in range(3):
            for v, out, back in moves(p, stage):
                out().wait_send()
    for j, out, back in shares:
        out.wait_send()


def grads(rt, dx):
    vmem = pl.BlockSpec(memory_space=pltpu.VMEM)
    V = pltpu.VMEM
    dma = pltpu.SemaphoreType.DMA
    return pl.pallas_call(
        grads_kernel,
        in_specs=[vmem] * 2,
        out_specs=[vmem] * 2,
        out_shape=[
            jax.ShapeDtypeStruct((128, D), F32),
            jax.ShapeDtypeStruct((128, 160), F32),
        ],
        scratch_shapes=[
            V((8, 128, T2), BF),
            V((PARTS, COLS, T2), BF),
            V((PARTS, 8, 128, COLS), F32),
            V((PARTS, 4, 4, 4, 16, COLS), BF),
            V((PARTS, 4, 4, 4, 16, COLS), BF),
            V((PARTS, 4, 4, 16, COLS), BF),
            V((PARTS, 4, 4, 16, COLS), BF),
            V((PARTS, 4, 16, COLS), F32),
            V((PARTS, 4, 16, COLS), F32),
            V((16, WIDE), BF),
            V((8, 16, WIDE), BF),
            dma((4,)),
            dma((4,)),
            dma((PARTS, 3, 4)),
            dma((PARTS, 3, 4)),
            dma((8,)),
            dma((8,)),
        ],
        compiler_params=pltpu.CompilerParams(
            collective_id=1, has_side_effects=True, vmem_limit_bytes=56 * 2**20
        ),
        name="grads",
    )(rt.reshape(8, 2, 128, T2), dx.reshape(PARTS, COLS, T2))


def shards(hidden, x_weight, state_weight, log_rates, step_bias, out_gain, cotangent):
    rt, xt, proj = project(hidden[0], x_weight, state_weight)
    mixed, dx = scan(
        xt, proj, cotangent[0], out_gain[None], log_rates[None], step_bias[None]
    )
    grad_x, grad_small = grads(rt, dx)
    return (mixed[None], grad_x, grad_small)


def solution(mesh):
    return jax.shard_map(
        shards,
        mesh=mesh,
        in_specs=(P("dp", "ctx", None), P(), P(), P(), P(), P(), P("dp", "ctx", None)),
        out_specs=(P("dp", "ctx", None), P("ctx", None), P("ctx", None)),
        check_vma=False,
    )
```

time: 1100 us -> 146 us (0.13)
  waiting for transfers between devices: 640 us -> 0 us
  Pallas kernels: 0 us -> 138 us
  local copies, waits for them, and re-layouts: 133 us -> 7.26 us
  matrix products: 121 us -> 0 us
  other arithmetic: 118 us -> 0 us
  blocking collectives: 45.8 us -> 0 us
  starting transfers between devices: 15.6 us -> 0 us
  between operations: 15.8 us -> 0.69 us
    all_gather x4 -> x0, waiting for transfers between devices: 220 us -> none  [carried_in(): everything = jax.tree.map(lambda part: lax.all_gather(part, axis), array)]
    ppermute x8 -> x0, waiting for transfers between devices: 197 us -> none  [swapped(): lax.ppermute(array, axis, [(i, i ^ 1 << apart) for i in range(lax.axis_si...]
    reduce_scatter x2 -> x0, waiting for transfers between devices: 146 us -> none  [the longest x1 146 us: shards(): lax.psum_scatter(term_x, 'ctx', scatter_dimension=0, tiled=True)]
    pallas_call x0 -> x3, Pallas kernels: none -> 138 us  [the longest x1 67.2 us: grads(): pl.pallas_call(grads_kernel, in_specs=[vmem] * 2, out_specs=[vmem] * 2, o...]
    dot_general x32 -> x0, matrix products: 121 us -> none  [the longest x6 51.3 us: forward_y(): inner = jnp.einsum('hts,shp->thp', mixing, per_head, precision=precise)]
    select_n x32 -> x0, other arithmetic: 79.8 us -> none  [step(): return jax.tree.map(lambda a, b: jnp.where(reached, a, b), new, before)]
    psum x1 -> x0, waiting for transfers between devices: 78.3 us -> none  [shards(): grad_x, grad_small = lax.psum((shard_x, shard_small), 'dp')]
    mul x65 -> x0, local copies, waits for them, and re-layouts: 61.3 us -> none  [the longest x64 60.6 us: chain(): later[0][:, None, None] * earlier[1] + later[1]]
  transfers between devices with their start and end apart: 15 -> 0, of which waited for: 13 -> 0; matrix products, arithmetic and copies ran while one was open for 15% -> 0% of each run, Pallas kernels for 0% -> 0%
where the time goes in v1:
time: 146 us
  Pallas kernels  138 us (95%)
  local copies, waits for them, and re-layouts  7.26 us (5%)
    pallas_call x1, Pallas kernels, grads(): pl.pallas_call(grads_kernel, in_specs=[vmem] * 2, out_specs=[vmem] * 2, o...  67.2 us
    pallas_call x1, Pallas kernels, scan(): pl.pallas_call(scan_kernel, in_specs=[vmem] * 6, out_specs=[vmem] * 2, ou...  59.4 us
    pallas_call x1, Pallas kernels, project(): pl.pallas_call(project_kernel, grid=(D // cols,), in_specs=[pl.BlockSpec(...  11.3 us
    unnamed x14, local copies, waits for them, and re-layouts  7.26 us

profile of v1, /device:TPU:0, one launch (start us, length us, event | category | flops | bytes accessed | tf_op | source)
XLA Modules:
  0.0 145.8 jit_solution(12192303213582808364)
XLA Ops:
  0.6 0.0 copy-start.1
  0.6 1.5 %copy.10.ws_ref = bf16[2048,160]{1,0:T(8,128)(2,1)S(1)} copy(bf16[2048,160]{0,1:T(8,128)(2,1)} %param.9) | data formatting | bytes 1310720 | tf_op args[2]
  2.1 0.0 copy-done.1
  2.2 11.3 %project.1 = (bf16[2048,512]{1,0:T(8,128)(2,1)S(1)}, bf16[2048,512]{1,0:T(8,128)(2,1)}, f32[512,256]{1,0:T(8,128)S(1)}) custom-call(bf16[256,2048]{1,0:T(8,128)(2,1)S(1)} %bitcast.9, bf16[2048,2048]{1,0:T(8,128)(2,1)} %wx_ref.1, bf16[2048,160]{1,0:T(8,128)(2,1)S(1)} %copy.10.ws_ref), custom_call_target="tpu_custom_call" | custom-call | tf_op jit(solution)/shard_map/project/pallas_call | solution.py:69
  13.5 0.0 copy-start
  13.5 1.3 copy-done
  14.8 0.0 copy-start.2
  14.8 0.8 copy-done.2
  15.6 59.4 %scan.1 = (bf16[256,2048]{1,0:T(8,128)(2,1)}, bf16[2304,512]{1,0:T(8,128)(2,1)}) custom-call(bf16[2048,512]{1,0:T(8,128)(2,1)} %get-tuple-element.10.xt_ref, f32[512,256]{1,0:T(8,128)} %copy-done.2, bf16[256,2048]{1,0:T(8,128)(2,1)} %bitcast.12, f32[1,2048]{1,0:T(1,128)} %bitcast.13, f32[1,32]{1,0:T(1,128)} %bitcast.14, f32[1,32]{1,0:T(1,128)} %bitcast.15), custom_call_target="tpu_custom_call" | custom-call | tf_op jit(solution)/shard_map/scan/pallas_call | solution.py:410
  75.0 0.0 copy-start.3
  75.0 67.2 %grads.1 = (f32[128,2048]{1,0:T(8,128)}, f32[128,160]{1,0:T(8,128)}) custom-call(bf16[8,2,128,512]{3,2,1,0:T(8,128)(2,1)} %bitcast.8, bf16[3,768,512]{2,1,0:T(8,128)(2,1)} %bitcast.10), custom_call_target="tpu_custom_call" | custom-call | tf_op jit(solution)/shard_map/grads/pallas_call | solution.py:604
  142.1 0.0 copy-start.4
  142.1 1.7 %copy.11 = f32[128,160]{0,1:T(8,128)} copy(f32[128,160]{1,0:T(8,128)} %get-tuple-element.19) | data formatting | bytes 163840
  143.9 0.0 copy-done.3
  143.9 1.0 copy.14
  144.8 0.0 copy-done.4
  144.9 1.0 copy.15
Async XLA Ops:
  0.6 1.5 %copy-start.1 = (bf16[1,256,2048]{2,1,0:T(8,128)(2,1)S(1)}, bf16[1,256,2048]{2,1,0:T(8,128)(2,1)}, u32[]{:S(2)}) copy-start(bf16[1,256,2048]{2,1,0:T(8,128)(2,1)} %param.7) | copy-start | bytes 3145732
  13.5 1.3 copy-start
  14.8 0.8 copy-start.2
  75.0 68.9 %copy-start.3 = (bf16[256,2048]{1,0:T(8,128)(2,1)S(1)}, bf16[256,2048]{1,0:T(8,128)(2,1)}, u32[]{:S(2)}) copy-start(bf16[256,2048]{1,0:T(8,128)(2,1)} %get-tuple-element.12) | copy-start | bytes 3145732
  142.1 2.7 %copy-start.4 = (f32[128,2048]{1,0:T(8,128)S(1)}, f32[128,2048]{1,0:T(8,128)}, u32[]{:S(2)}) copy-start(f32[128,2048]{1,0:T(8,128)} %get-tuple-element.24) | copy-start | bytes 3145732

commit v2 on v1

--- a/solution.py
+++ b/solution.py
@@ -15,7 +15,7 @@
 PEERS = 16
 SLOT = 144
 WIDE = 2304
-PARTS = 3
+PARTS = 6
 COLS = WIDE // PARTS
 MESH = pl.DeviceIdType.MESH
 BF = jnp.bfloat16
@@ -198,7 +198,7 @@
         send_a[hp, 128:144, :] = extra.astype(BF)
         return c
 
-    lax.fori_loop(0, PAIRS, local_end, 0)
+    lax.fori_loop(0, PAIRS, local_end, 0, unroll=4)
     recv_a[me] = send_a[me]
     pl.semaphore_wait(barrier, PEERS - 1)
     send_all(send_a, recv_a, sa, ra)
@@ -288,7 +288,7 @@
         return q, e
 
     none = jnp.zeros((1, T2), F32)
-    q, e = lax.fori_loop(0, PAIRS, readout, (none, none))
+    q, e = lax.fori_loop(0, PAIRS, readout, (none, none), unroll=4)
     scale = lax.rsqrt(q * (1.0 / D) + 1e-05)
     pull = scale * scale * scale * e * (1.0 / D)
 
@@ -310,7 +310,7 @@
         send_b[hp] = to_state(vdu[pl.ds(base, 128), :], bdc)
         return c
 
-    lax.fori_loop(0, PAIRS, normed, 0)
+    lax.fori_loop(0, PAIRS, normed, 0, unroll=4)
     recv_b[me] = send_b[me]
     send_all(send_b, recv_b, sb, rb)
     dsc[...] = jnp.zeros_like(dsc)
@@ -348,7 +348,7 @@
     def read_maps(hp, acc):
         return acc + dot(recv_a2[hp], vdu[pl.ds(pl.multiple_of(hp * 128, 128), 128), :], TN)
 
-    dc_state = lax.fori_loop(0, PAIRS, read_maps, jnp.zeros((128, T2), F32))
+    dc_state = lax.fori_loop(0, PAIRS, read_maps, jnp.zeros((128, T2), F32), unroll=4)
 
     recv_all(send_b2, recv_b2, sb2, rb2)
 
@@ -371,7 +371,7 @@
             q2row[h, :] = jnp.sum(x * far, axis=0, keepdims=True)
         return acc
 
-    db_state = lax.fori_loop(0, PAIRS, finish, jnp.zeros((128, T2), F32))
+    db_state = lax.fori_loop(0, PAIRS, finish, jnp.zeros((128, T2), F32), unroll=4)
 
     met = asrow[...] * tot[...]
     neg_col = jnp.broadcast_to(neg_rate, (128, 128)).T[0:HEADS, 0:1]
@@ -389,10 +389,13 @@
         ratio = jnp.where(zb < -20.0, 1.0, sig / step_t[:, lanes])
         dz = qrow[:, lanes] * ratio + da * neg_col * sig
         dxt_ref[D + 128 : D + 160, lanes] = dz.astype(BF)
-        d_scores = jnp.where(causal[b], dsc[b], 0.0).astype(BF)
+        d_scores = jnp.where(causal[b], dsc[b], 0.0)
         part = slice(b * 64, b * 64 + 64)
-        dc = dot(bdbt[part, lanes], d_scores, NT) + dc_state[part, lanes]
-        db = dot(bdct[part, lanes], d_scores) + db_state[part, lanes]
+        fine = slice(128 + b * 64, 192 + b * 64)
+        own_b = bdbt[part, lanes].astype(F32) + bdbt[fine, lanes].astype(F32)
+        own_c = bdct[part, lanes].astype(F32) + bdct[fine, lanes].astype(F32)
+        dc = dot_exact(own_b, d_scores, NT) + dc_state[part, lanes]
+        db = dot_exact(own_c, d_scores) + db_state[part, lanes]
         dxt_ref[D : D + 64, lanes] = db.astype(BF)
         dxt_ref[D + 64 : D + 128, lanes] = dc.astype(BF)
 
@@ -455,7 +458,7 @@
 
 def grads_kernel(
     rt_ref, dx_ref, gx_ref, gs_ref,
-    rt_in, dx_in, acc, buf1, in1, buf2, in2, buf3, in3, last, out_in,
+    rt_in, dx_in, acc, buf1, in1, buf2, in2, buf3, in3, last0, last1, last2, out0, out1, out2,
     core_s, core_r, ss, rs, out_s, out_r,
 ):
     dp = lax.axis_index("dp")
@@ -488,7 +491,7 @@
             device_id=friend, device_id_type=MESH,
         )
 
-    swaps = [to(sibling, rt_ref.at[:, 1 - core], rt_in, core_s.at[3], core_r.at[3])]
+    swaps = [to(sibling, rt_ref.at[:, 1 - core], rt_in, core_s.at[PARTS], core_r.at[PARTS])]
     swaps += [
         to(sibling, dx_ref.at[p], dx_in.at[p], core_s.at[p], core_r.at[p])
         for p in range(PARTS)
@@ -496,13 +499,13 @@
     for swap in swaps:
         swap.start()
 
-    for p in range(PARTS):
-        def own(jj, c, p=p):
-            acc[p, jj] = dot(rt_ref[jj, core], dx_ref[p], NT)
-            return c
-        lax.fori_loop(0, 8, own, 0)
-
-    orders = (("z", "y", "x"), ("y", "x", "z"), ("x", "z", "y"))
+    def own(p, c):
+        acc[p] = dot(rt_ref[:, core].reshape(1024, T2), dx_ref[p], NT)
+        return c
+
+    lax.fori_loop(0, PARTS, own, 0)
+
+    orders = (("z", "y", "x"), ("y", "x", "z"), ("x", "z", "y")) * 2
     stages = ((buf1, in1), (buf2, in2), (buf3, in3))
 
     def moves(p, stage):
@@ -540,52 +543,87 @@
     for p in range(PARTS):
         swaps[1 + p].wait_recv()
 
-        def both(jj, c, p=p):
-            tile = (acc[p, jj] + dot(rt_in[jj], dx_in[p], NT)).astype(BF)
-            y_to, x_lo_to = jj // 2, jj % 2
-            for k in range(8):
-                where = {"z": k // 2, "y": y_to, "x": (k % 2) * 2 + x_lo_to}
-                a, b, d = (where[axis] for axis in orders[p])
-                buf1[p, a, b, d] = tile[k * 16 : (k + 1) * 16]
-            return c
-        lax.fori_loop(0, 8, both, 0)
+        tile = (acc[p] + dot(rt_in[...].reshape(1024, T2), dx_in[p], NT)).astype(BF)
+        for k in range(64):
+            jj, m = k // 8, k % 8
+            where = {"z": m // 2, "y": jj // 2, "x": (m % 2) * 2 + jj % 2}
+            a, b, d = (where[axis] for axis in orders[p])
+            buf1[p, a, b, d] = tile[k * 16 : (k + 1) * 16]
         launch(p, 0)
 
-    for p in range(PARTS):
+    def first(p):
         found = moves(p, 0)
         for v, out, back in found:
             back().wait_recv()
         here = coords[orders[p][0]]
 
-        def add(i, c, p=p, here=here, found=found):
+        def add(i, c):
             total = buf1[p, here, i].astype(F32)
             for v, out, back in found:
                 total = total + in1[p, v, i].astype(F32)
             buf2[p, i] = total.astype(BF)
             return c
+
         lax.fori_loop(0, 4, add, 0)
         launch(p, 1)
-    for p in range(PARTS):
+
+    def second(p):
         buf3[p] = collect(p, 1)
         launch(p, 2)
-    for p in range(PARTS):
-        last[:, p * COLS : (p + 1) * COLS] = collect(p, 2).astype(BF)
-
+
+    half = PARTS // 2
+    groups = (range(half), range(half, PARTS))
     shares = []
-    for k in range(1, 8):
-        j = (dp + k) % 8
-        friend = {"dp": j, "ctx": ctx}
-        out = to(friend, last, out_in.at[dp], out_s.at[j], out_r.at[dp])
-        back = to(friend, last, out_in.at[j], out_s.at[j], out_r.at[j])
-        out.start()
-        shares.append((j, out, back))
-    out_in[dp] = last[...]
-    for j, out, back in shares:
-        back.wait_recv()
-    for k in range(8):
-        piece = out_in[k].astype(F32)
-        gx_ref[k * 16 : (k + 1) * 16, :] = piece[:, 0:D]
-        gs_ref[k * 16 : (k + 1) * 16, :] = piece[:, D : D + 160]
+
+    def share(kind, src, dst):
+        dst[dp] = src[...]
+        for k in range(1, 8):
+            j = (dp + k) % 8
+
+            def copy(slot, j=j):
+                return to(
+                    {"dp": j, "ctx": ctx}, src, dst.at[slot],
+                    out_s.at[kind, j], out_r.at[kind, slot],
+                )
+
+            copy(dp).start()
+            shares.append((kind, j, lambda copy=copy: copy(dp), lambda copy=copy, j=j: copy(j)))
+
+    for group in groups:
+        for p in group:
+            first(p)
+    for group in groups:
+        for p in group:
+            second(p)
+    for p in groups[0]:
+        last0[:, p * COLS : (p + 1) * COLS] = collect(p, 2).astype(BF)
+    share(0, last0, out0)
+    for p in groups[1]:
+        piece = collect(p, 2)
+        at0 = (p - half) * COLS
+        if p == PARTS - 1:
+            last2[...] = piece[:, COLS - 256 :]
+            piece = piece[:, : COLS - 256]
+        last1[:, at0 : at0 + piece.shape[1]] = piece.astype(BF)
+    share(2, last2, out2)
+    share(1, last1, out1)
+
+    def arrived(kind):
+        for which, j, out, back in shares:
+            if which == kind:
+                back().wait_recv()
+
+    edge = half * COLS
+    for kind, dst in ((0, out0), (2, out2), (1, out1)):
+        arrived(kind)
+        for k in range(8):
+            rows = slice(k * 16, (k + 1) * 16)
+            if kind == 0:
+                gx_ref[rows, 0:edge] = dst[k].astype(F32)
+            elif kind == 1:
+                gx_ref[rows, edge:D] = dst[k].astype(F32)
+            else:
+                gs_ref[rows, :] = dst[k][:, 0:160]
 
     for swap in swaps:
         swap.wait_send()
@@ -593,8 +631,8 @@
         for stage in range(3):
             for v, out, back in moves(p, stage):
                 out().wait_send()
-    for j, out, back in shares:
-        out.wait_send()
+    for which, j, out, back in shares:
+        out().wait_send()
 
 
 def grads(rt, dx):
@@ -612,21 +650,25 @@
         scratch_shapes=[
             V((8, 128, T2), BF),
             V((PARTS, COLS, T2), BF),
-            V((PARTS, 8, 128, COLS), F32),
+            V((PARTS, 1024, COLS), F32),
             V((PARTS, 4, 4, 4, 16, COLS), BF),
             V((PARTS, 4, 4, 4, 16, COLS), BF),
             V((PARTS, 4, 4, 16, COLS), BF),
             V((PARTS, 4, 4, 16, COLS), BF),
             V((PARTS, 4, 16, COLS), F32),
             V((PARTS, 4, 16, COLS), F32),
-            V((16, WIDE), BF),
-            V((8, 16, WIDE), BF),
-            dma((4,)),
-            dma((4,)),
+            V((16, WIDE // 2), BF),
+            V((16, WIDE // 2 - 256), BF),
+            V((16, 256), F32),
+            V((8, 16, WIDE // 2), BF),
+            V((8, 16, WIDE // 2 - 256), BF),
+            V((8, 16, 256), F32),
+            dma((PARTS + 1,)),
+            dma((PARTS + 1,)),
             dma((PARTS, 3, 4)),
             dma((PARTS, 3, 4)),
-            dma((8,)),
-            dma((8,)),
+            dma((3, 8)),
+            dma((3, 8)),
         ],
         compiler_params=pltpu.CompilerParams(
             collective_id=1, has_side_effects=True, vmem_limit_bytes=56 * 2**20

time: 146 us -> 125 us (0.86)
  Pallas kernels: 138 us -> 116 us
    pallas_call x1, Pallas kernels: 67.2 us -> 52.4 us  [grads(): pl.pallas_call(grads_kernel, in_specs=[vmem] * 2, out_specs=[vmem] * 2, o...]
    pallas_call x1, Pallas kernels: 59.4 us -> 52.4 us  [scan(): pl.pallas_call(scan_kernel, in_specs=[vmem] * 6, out_specs=[vmem] * 2, ou...]
where the time goes in v2:
time: 125 us; the launch traced here: 124 us
  Pallas kernels  116 us (93%)
  local copies, waits for them, and re-layouts  7.26 us (6%)
    pallas_call x1, Pallas kernels, scan(): pl.pallas_call(scan_kernel, in_specs=[vmem] * 6, out_specs=[vmem] * 2, ou...  52.4 us
    pallas_call x1, Pallas kernels, grads(): pl.pallas_call(grads_kernel, in_specs=[vmem] * 2, out_specs=[vmem] * 2, o...  52.4 us
    pallas_call x1, Pallas kernels, project(): pl.pallas_call(project_kernel, grid=(D // cols,), in_specs=[pl.BlockSpec(...  11.3 us
    unnamed x14, local copies, waits for them, and re-layouts  7.26 us

profile of v2, /device:TPU:0, one launch (start us, length us, event | category | flops | bytes accessed | tf_op | source)
XLA Modules:
  0.0 124.1 jit_solution(10941489177991793693)
XLA Ops:
  0.6 0.0 copy-start.1
  0.6 1.5 %copy.10.ws_ref = bf16[2048,160]{1,0:T(8,128)(2,1)S(1)} copy(bf16[2048,160]{0,1:T(8,128)(2,1)} %param.9) | data formatting | bytes 1310720 | tf_op args[2]
  2.1 0.0 copy-done.1
  2.2 11.3 %project.1 = (bf16[2048,512]{1,0:T(8,128)(2,1)S(1)}, bf16[2048,512]{1,0:T(8,128)(2,1)}, f32[512,256]{1,0:T(8,128)S(1)}) custom-call(bf16[256,2048]{1,0:T(8,128)(2,1)S(1)} %bitcast.9, bf16[2048,2048]{1,0:T(8,128)(2,1)} %wx_ref.1, bf16[2048,160]{1,0:T(8,128)(2,1)S(1)} %copy.10.ws_ref), custom_call_target="tpu_custom_call" | custom-call | tf_op jit(solution)/shard_map/project/pallas_call | solution.py:69
  13.5 0.0 copy-start
  13.5 1.3 %copy-done = bf16[2048,512]{1,0:T(8,128)(2,1)} copy-done((bf16[2048,512]{1,0:T(8,128)(2,1)}, bf16[2048,512]{1,0:T(8,128)(2,1)S(1)}, u32[]{:S(2)}) %copy-start) | copy-done | bytes 2097176
  14.8 0.0 copy-start.2
  14.8 0.8 copy-done.2
  15.6 52.4 %scan.1 = (bf16[256,2048]{1,0:T(8,128)(2,1)}, bf16[2304,512]{1,0:T(8,128)(2,1)}) custom-call(bf16[2048,512]{1,0:T(8,128)(2,1)} %get-tuple-element.10.xt_ref, f32[512,256]{1,0:T(8,128)} %copy-done.2, bf16[256,2048]{1,0:T(8,128)(2,1)} %bitcast.12, f32[1,2048]{1,0:T(1,128)} %bitcast.13, f32[1,32]{1,0:T(1,128)} %bitcast.14, f32[1,32]{1,0:T(1,128)} %bitcast.15), custom_call_target="tpu_custom_call" | custom-call | tf_op jit(solution)/shard_map/scan/pallas_call | solution.py:413
  68.0 0.0 copy-start.3
  68.0 52.4 %grads.1 = (f32[128,2048]{1,0:T(8,128)}, f32[128,160]{1,0:T(8,128)}) custom-call(bf16[8,2,128,512]{3,2,1,0:T(8,128)(2,1)} %bitcast.8, bf16[6,384,512]{2,1,0:T(8,128)(2,1)} %bitcast.10), custom_call_target="tpu_custom_call" | custom-call | tf_op jit(solution)/shard_map/grads/pallas_call | solution.py:642
  120.4 0.0 copy-start.4
  120.5 1.7 %copy.11 = f32[128,160]{0,1:T(8,128)} copy(f32[128,160]{1,0:T(8,128)} %get-tuple-element.19) | data formatting | bytes 163840
  122.2 0.0 copy-done.3
  122.2 1.0 copy.14
  123.2 0.0 copy-done.4
  123.2 1.0 copy.15
Async XLA Ops:
  0.6 1.5 %copy-start.1 = (bf16[1,256,2048]{2,1,0:T(8,128)(2,1)S(1)}, bf16[1,256,2048]{2,1,0:T(8,128)(2,1)}, u32[]{:S(2)}) copy-start(bf16[1,256,2048]{2,1,0:T(8,128)(2,1)} %param.7) | copy-start | bytes 3145732
  13.5 1.3 %copy-start = (bf16[2048,512]{1,0:T(8,128)(2,1)}, bf16[2048,512]{1,0:T(8,128)(2,1)S(1)}, u32[]{:S(2)}) copy-start(bf16[2048,512]{1,0:T(8,128)(2,1)S(1)} %get-tuple-element.13) | copy-start | bytes 6291460
  14.8 0.8 copy-start.2
  68.0 54.1 %copy-start.3 = (bf16[256,2048]{1,0:T(8,128)(2,1)S(1)}, bf16[256,2048]{1,0:T(8,128)(2,1)}, u32[]{:S(2)}) copy-start(bf16[256,2048]{1,0:T(8,128)(2,1)} %get-tuple-element.12) | copy-start | bytes 3145732
  120.4 2.7 %copy-start.4 = (f32[128,2048]{1,0:T(8,128)S(1)}, f32[128,2048]{1,0:T(8,128)}, u32[]{:S(2)}) copy-start(f32[128,2048]{1,0:T(8,128)} %get-tuple-element.24) | copy-start | bytes 3145732

commit v3 on v1

v3 whole, which is shorter than its diff:
```python
import jax
import jax.numpy as jnp
from jax import lax
from jax.experimental import pallas as pl
from jax.experimental.pallas import tpu as pltpu
from jax.sharding import PartitionSpec as P

HEAD = 64
STATE = 64
D = 2048
ROWS = 256
T2 = 2 * ROWS
HEADS = 32
PAIRS = 16
PEERS = 16
SLOT = 144
WIDE = 2304
COLS = 256
PARTS = WIDE // COLS
MESH = pl.DeviceIdType.MESH
BF = jnp.bfloat16
F32 = jnp.float32
LOG2E = 1.4426950408889634

NN = (((1,), (0,)), ((), ()))
NT = (((1,), (1,)), ((), ()))
TN = (((0,), (0,)), ((), ()))


def dot(a, b, dims=NN):
    return lax.dot_general(a, b, dims, preferred_element_type=F32)


def dot_exact(a, b, dims=NN):
    return lax.dot_general(
        a, b, dims, preferred_element_type=F32, precision=lax.Precision.HIGHEST
    )


def iota2(shape, dim):
    return lax.broadcasted_iota(jnp.int32, shape, dim)


def flip_matrix(n):
    return (iota2((n, n), 0) + iota2((n, n), 1) == n - 1).astype(F32).astype(BF)


def scan_kernel(
    rows_ref, w_hbm, wst_ref, cot_ref, gain_ref, lr_ref, sb_ref,
    mixed_ref, gx_ref, gs_ref,
    xt_ref, proj_ref, w_sem,
    small, zt, step_t, weight, l2_t, l2_n, el_t, bdb, bdbt, bdc, bdct, scm, dsc,
    wx, ct, u, g, du, vdu, mst, dec, tot, prow, qrow, q2row, asrow,
    send_a, recv_a, send_a2, recv_a2, send_b, recv_b, send_b2, recv_b2, up,
    rt_in, dx_in, in1, in2, buf3, in3, last, last2, outs, out2,
    sa, ra, sa2, ra2, sb, rb, sb2, rb2, core_s, core_r, ss, rs, out_s, out_r,
):
    me = lax.axis_index("ctx")
    dp = lax.axis_index("dp")
    chip, core = me // 2, me % 2
    zz, x_hi = dp // 2, dp % 2
    yy, x_lo = chip // 2, chip % 2
    xx = x_hi * 2 + x_lo
    coords = {"z": zz, "y": yy, "x": xx}
    sibling = {"dp": dp, "ctx": chip * 2 + (1 - core)}
    dx = du

    def at_axis(axis, v):
        if axis == "z":
            return {"dp": v * 2 + x_hi, "ctx": me}
        if axis == "y":
            return {"dp": dp, "ctx": (v * 2 + x_lo) * 2 + core}
        return {"dp": zz * 2 + v // 2, "ctx": (yy * 2 + v % 2) * 2 + core}

    def to(friend, src, dst, ssem, rsem):
        return pltpu.make_async_remote_copy(
            src_ref=src, dst_ref=dst, send_sem=ssem, recv_sem=rsem,
            device_id=friend, device_id_type=MESH,
        )

    barrier = pltpu.get_barrier_semaphore()

    def w_block(j):
        return pltpu.make_async_copy(
            w_hbm.at[:, pl.ds(pl.multiple_of(j * 256, 256), 256)],
            dec.at[pl.ds(pl.multiple_of(j * D, D), D), :],
            w_sem.at[j],
        )

    turns = [lax.rem(chip + k, 8) for k in range(8)]
    for j in turns:
        w_block(j).start()

    friends = [{"dp": dp, "ctx": (me + k) % PEERS} for k in range(1, PEERS)]
    friends += [{"dp": (dp + k) % 8, "ctx": me} for k in range(1, 8)]
    friends += [{"dp": zz * 2 + (1 - x_hi), "ctx": (yy * 2 + (1 - x_lo)) * 2 + core}]
    for friend in friends:
        pl.semaphore_signal(barrier, inc=1, device_id=friend, device_id_type=MESH)

    def copy(src, dst, ssem, rsem, peer, slot):
        return pltpu.make_async_remote_copy(
            src_ref=src.at[peer], dst_ref=dst.at[slot], send_sem=ssem.at[peer],
            recv_sem=rsem.at[slot], device_id={"dp": dp, "ctx": peer}, device_id_type=MESH,
        )

    def send_all(src, dst, ssem, rsem):
        def one(k, c):
            j = lax.rem(me + k, PEERS)
            copy(src, dst, ssem, rsem, j, me).start()
            return c
        lax.fori_loop(1, PEERS, one, 0)

    def recv_all(src, dst, ssem, rsem):
        def one(k, c):
            j = lax.rem(me + k, PEERS)
            copy(src, dst, ssem, rsem, j, j).wait_recv()
            return c
        lax.fori_loop(1, PEERS, one, 0)

    def sent_all(src, dst, ssem, rsem):
        def one(k, c):
            j = lax.rem(me + k, PEERS)
            copy(src, dst, ssem, rsem, j, me).wait_send()
            return c
        lax.fori_loop(1, PEERS, one, 0)

    low = iota2((1, 128), 1) < 64
    row_i = iota2((ROWS, ROWS), 0)
    col_i = iota2((ROWS, ROWS), 1)
    causal = (row_i >= col_i, row_i <= col_i)
    tri = [m.astype(F32) for m in causal]
    halves = (slice(0, ROWS), slice(ROWS, T2))

    flip = flip_matrix(256)
    for k in range(8):
        part = rows_ref[:, k * 256 : (k + 1) * 256]
        mst[k * T2 : k * T2 + ROWS, :] = part
        mst[(7 - k) * T2 + ROWS : (8 - k) * T2, :] = dot(part, flip).astype(BF)

    def both_rows():
        return jnp.concatenate([mst[k * T2 : (k + 1) * T2, :] for k in range(8)], axis=1)

    proj_ref[:, 160:256] = jnp.zeros((T2, 96), F32)
    proj_ref[:, 0:160] = dot(both_rows(), wst_ref[...], NT)
    small[...] = jnp.zeros_like(small)
    small[0:1, 0:HEADS] = -jnp.exp(lr_ref[...])
    small[1:2, 0:HEADS] = sb_ref[...]
    neg_rate = small[0:1, :]
    z = proj_ref[:, 128:256] + small[1:2, :]
    step_n = jnp.maximum(z, 0.0) + jnp.log1p(jnp.exp(-jnp.abs(z)))
    log_n = step_n * (neg_rate * LOG2E)
    zt[...] = z.T[0:HEADS]
    step_t[...] = step_n.T[0:HEADS]
    for b in range(2):
        l2 = dot_exact(tri[b], log_n[halves[b]])
        l2_n[b] = l2
        l2_t[:, halves[b]] = l2.T[0:HEADS]
    el_t[...] = jnp.exp2(l2_t[...])
    ends = (l2_t[:, ROWS - 1 : ROWS], l2_t[:, ROWS : ROWS + 1])
    tot[...] = jnp.exp2(jnp.where(low, ends[0], ends[1]))
    for b in range(2):
        weight[:, halves[b]] = step_t[:, halves[b]] * jnp.exp2(ends[b] - l2_t[:, halves[b]])

    both = proj_ref[:, 0:128]
    turned = pltpu.roll(both, 64, 1)
    own = (iota2((T2, 128), 0) < ROWS) == (iota2((T2, 128), 1) < 64)
    maps_b = jnp.where(low, both, turned)
    maps_c = jnp.where(low, turned, both)
    b_diag = jnp.where(own, maps_b, 0.0)
    c_diag = jnp.where(own, maps_c, 0.0)
    for full, by_rows, by_cols in ((b_diag, bdb, bdbt), (c_diag, bdc, bdct)):
        coarse = full.astype(BF).astype(F32)
        for k, term in enumerate((coarse, full - coarse)):
            by_rows[:, k * 128 : (k + 1) * 128] = term.astype(BF)
            by_cols[k * 128 : (k + 1) * 128, :] = term.T.astype(BF)

    def to_state(lhs, by_rows):
        out = dot(lhs, by_rows[...])
        return (out[:, 0:128] + out[:, 128:256]).astype(BF)

    def from_state(state, by_cols):
        return dot(jnp.concatenate([state, state], axis=1), by_cols[...])

    def local_end(hp, c):
        base = pl.multiple_of(hp * 128, 128)
        for hh in range(2):
            rows = pl.ds(pl.multiple_of(base + hh * 64, 64), 64)
            h = pl.ds(2 * hp + hh, 1)
            wx[rows, :] = (xt_ref[rows, :].astype(F32) * weight[h, :]).astype(BF)
        send_a[hp, 0:128, :] = to_state(wx[pl.ds(base, 128), :], bdb)
        t0 = tot[pl.ds(2 * hp, 1), :]
        t1 = tot[pl.ds(2 * hp + 1, 1), :]
        h0 = t0.astype(BF).astype(F32)
        h1 = t1.astype(BF).astype(F32)
        at = iota2((16, 128), 0)
        extra = jnp.where(at == 0, h0, jnp.where(at == 1, t0 - h0, jnp.where(at == 2, h1, t1 - h1)))
        send_a[hp, 128:144, :] = extra.astype(BF)
        return c

    def early(step, src, dst, ssem, rsem):
        def one(k, c):
            j = lax.rem(me + k, PEERS)
            step(j, 0)
            copy(src, dst, ssem, rsem, j, me).start()
            return c
        lax.fori_loop(1, PEERS, one, 0, unroll=5)
        step(me, 0)
        dst[me] = src[me]

    pl.semaphore_wait(barrier, len(friends))
    for k, j in enumerate(turns):
        w_block(j).wait()
        values = dot(both_rows(), dec[pl.ds(pl.multiple_of(j * D, D), D), :]).astype(BF)
        xt_ref[pl.ds(pl.multiple_of(j * 256, 256), 256), :] = values.T
        if k == 0:
            hp = sibling["ctx"]
            local_end(hp, 0)
            copy(send_a, recv_a, sa, ra, hp, me).start()
            local_end(me, 0)
            recv_a[me] = send_a[me]
        else:
            for hh in range(2):
                hp = 2 * j + hh
                local_end(hp, 0)
                copy(send_a, recv_a, sa, ra, hp, me).start()

    for b in range(2):
        sc = dot_exact(
            jnp.where(low, maps_c[halves[b]], 0.0), maps_b[halves[b]], NT
        )
        scm[b] = jnp.where(causal[b], sc, 0.0)

    zero_half = jnp.zeros((128, 128), BF)
    blocks = (((0, 0), (1, 0), (1, 1)), ((0, 0), (0, 1), (1, 1)))

    def span(i):
        return slice(i * 128, (i + 1) * 128)

    def tile(b, h, i, rows=128):
        return pl.ds(pl.multiple_of((b * HEADS + h) * ROWS + i * 128, 128), rows)

    def forward(hp, c):
        for hh in range(2):
            h = 2 * hp + hh
            rows = pl.ds(pl.multiple_of(h * 64, 64), 64)
            for b in range(2):
                column = pltpu.roll(l2_n[b], 128 - h, 1)[:, 0:1]
                line = l2_t[pl.ds(h, 1), halves[b]]
                size = step_t[pl.ds(h, 1), halves[b]]
                for i, j in blocks[b]:
                    d = jnp.exp2(jnp.minimum(column[span(i)] - line[:, span(j)], 0.0))
                    d = d * size[:, span(j)]
                    dec[tile(b, h, i), span(j)] = d.astype(BF)
                    mst[tile(b, h, i), span(j)] = (d * scm[b, span(i), span(j)]).astype(BF)
                mst[tile(b, h, b), span(1 - b)] = zero_half
                u[rows, halves[b]] = dot(xt_ref[rows, halves[b]], mst[tile(b, h, 0, ROWS), :], NT)
        return c

    def chain(recv, out, fwd_up):
        def totals(i):
            t = recv_a[i, 128:144, :].astype(F32)
            rows = iota2((128, 128), 0) < 64
            return jnp.where(rows, t[0:1] + t[1:2], t[2:3] + t[3:4])

        def climb(i, carry):
            up[i] = carry
            return totals(i) * carry + recv[i, 0:128, :].astype(F32)

        zero = jnp.zeros((128, 128), F32)
        lax.fori_loop(0, PEERS, climb, zero)

        def descend(k, carry):
            i = PEERS - 1 - k
            pick = low if fwd_up else jnp.logical_not(low)
            out[i] = jnp.where(pick, up[i], carry).astype(BF)
            return totals(i) * carry + recv[i, 0:128, :].astype(F32)

        lax.fori_loop(0, PEERS, descend, zero)

    lax.fori_loop(0, PAIRS // 2, forward, 0)
    recv_all(send_a, recv_a, sa, ra)
    chain(recv_a, send_a2, True)
    recv_a2[me] = send_a2[me]
    send_all(send_a2, recv_a2, sa2, ra2)
    lax.fori_loop(PAIRS // 2, PAIRS, forward, 0)

    for blk in range(8):
        turned_c = cot_ref[:, blk * 256 : (blk + 1) * 256].T
        flipped_c = dot(flip, turned_c).astype(BF)
        for hh in range(2):
            ct[blk, hh, :, 0:ROWS] = turned_c[hh * 128 : hh * 128 + 128]
            ct[7 - blk, hh, :, ROWS:T2] = flipped_c[hh * 128 : hh * 128 + 128]

    recv_all(send_a2, recv_a2, sa2, ra2)

    def gains(hp):
        lane = pl.ds(pl.multiple_of(hp * 128, 128), 128)
        column = jnp.broadcast_to(gain_ref[:, lane], (128, 128)).T
        return jnp.concatenate([column] * 4, axis=1)

    def readout(hp, c):
        q, e = c
        base = pl.multiple_of(hp * 128, 128)
        out = from_state(recv_a2[hp], bdct)
        gain = gains(hp)
        for hh in range(2):
            rows = pl.ds(pl.multiple_of(base + hh * 64, 64), 64)
            part = slice(hh * 64, hh * 64 + 64)
            v = u[rows, :] + out[part] * el_t[pl.ds(2 * hp + hh, 1), :]
            u[rows, :] = v
            q = q + jnp.sum(v * v, axis=0, keepdims=True)
            e = e + jnp.sum(v * gain[part] * ct[lax.div(hp, 2), lax.rem(hp, 2), part, :].astype(F32), axis=0, keepdims=True)
        return q, e

    none = jnp.zeros((1, T2), F32)
    q, e = lax.fori_loop(0, PAIRS, readout, (none, none), unroll=4)
    scale = lax.rsqrt(q * (1.0 / D) + 1e-05)
    pull = scale * scale * scale * e * (1.0 / D)

    def normed(hp, c):
        base = pl.multiple_of(hp * 128, 128)
        gain = gains(hp)
        for hh in range(2):
            rows = pl.ds(pl.multiple_of(base + hh * 64, 64), 64)
            h = pl.ds(2 * hp + hh, 1)
            part = slice(hh * 64, hh * 64 + 64)
            v = u[rows, :]
            gs = gain[part] * scale
            back = gs * ct[lax.div(hp, 2), lax.rem(hp, 2), part, :].astype(F32) - v * pull
            vdu[rows, :] = (back * el_t[h, :]).astype(BF)
            back = back.astype(BF)
            du[rows, :] = back
            prow[h, :] = jnp.sum(back.astype(F32) * v, axis=0, keepdims=True)
            u[rows, :] = v * gs
        send_b[hp] = to_state(vdu[pl.ds(base, 128), :], bdc)
        return c

    early(normed, send_b, recv_b, sb, rb)
    dsc[...] = jnp.zeros_like(dsc)

    def backward(hp, c):
        for b in range(2):
            pair = []
            for hh in range(2):
                h = 2 * hp + hh
                rows = pl.ds(pl.multiple_of(h * 64, 64), 64)
                d = du[rows, halves[b]]
                g[rows, halves[b]] = dot(d, mst[tile(b, h, 0, ROWS), :])
                pair.append(dot(d, xt_ref[rows, halves[b]], TN))
            for i, j in blocks[b]:
                acc = dsc[b, span(i), span(j)]
                for hh in range(2):
                    acc = acc + pair[hh][span(i), span(j)] * dec[
                        tile(b, 2 * hp + hh, i), span(j)
                    ].astype(F32)
                dsc[b, span(i), span(j)] = acc
        return c

    lax.fori_loop(0, PAIRS // 2, backward, 0)
    for blk in range(8):
        y_rc = u[(7 - blk) * 256 : (8 - blk) * 256, ROWS:T2].astype(BF)
        y = u[blk * 256 : (blk + 1) * 256, 0:ROWS] + dot(flip, y_rc)
        mixed_ref[:, blk * 256 : (blk + 1) * 256] = y.astype(BF).T

    def read_maps(hp, acc):
        return acc + dot(recv_a2[hp], vdu[pl.ds(pl.multiple_of(hp * 128, 128), 128), :], TN)

    dc_state = lax.fori_loop(0, PAIRS, read_maps, jnp.zeros((128, T2), F32), unroll=4)
    recv_all(send_b, recv_b, sb, rb)
    chain(recv_b, send_b2, False)
    recv_b2[me] = send_b2[me]
    send_all(send_b2, recv_b2, sb2, rb2)
    lax.fori_loop(PAIRS // 2, PAIRS, backward, 0)

    own_maps = []
    for b in range(2):
        lanes = halves[b]
        d_scores = jnp.where(causal[b], dsc[b], 0.0)
        part = slice(b * 64, b * 64 + 64)
        fine = slice(128 + b * 64, 192 + b * 64)
        own_b = bdbt[part, lanes].astype(F32) + bdbt[fine, lanes].astype(F32)
        own_c = bdct[part, lanes].astype(F32) + bdct[fine, lanes].astype(F32)
        dc = dot_exact(own_b, d_scores, NT) + dc_state[part, lanes]
        dx[D + 64 : D + 128, lanes] = dc.astype(BF)
        own_maps.append(dot_exact(own_c, d_scores))
    dx[D + 160 : WIDE, :] = jnp.zeros((WIDE - D - 160, T2), BF)
    for blk in range(8):
        across = rows_ref[:, blk * 256 : (blk + 1) * 256].T
        flipped = dot(flip, across).astype(BF)
        for hh in range(2):
            ct[blk, hh, :, 0:ROWS] = across[hh * 128 : hh * 128 + 128]
            ct[7 - blk, hh, :, ROWS:T2] = flipped[hh * 128 : hh * 128 + 128]
    rows_swap = to(sibling, ct.at[:, 1 - core], rt_in, core_s.at[PARTS], core_r.at[PARTS])
    rows_swap.start()

    def swap(p):
        return to(
            sibling, dx.at[pl.ds(p * COLS, COLS), :], dx_in.at[p], core_s.at[p], core_r.at[p]
        )

    recv_all(send_b2, recv_b2, sb2, rb2)

    def finish(hp, acc):
        base = pl.multiple_of(hp * 128, 128)
        after = recv_b2[hp]
        acc = acc + dot(after, wx[pl.ds(base, 128), :], TN)
        out = from_state(after, bdbt)
        meet = after.astype(F32) * recv_a2[hp].astype(F32)
        for hh in range(2):
            rows = pl.ds(pl.multiple_of(base + hh * 64, 64), 64)
            h = pl.ds(2 * hp + hh, 1)
            part = slice(hh * 64, hh * 64 + 64)
            asrow[h, :] = jnp.sum(meet[part], axis=0, keepdims=True)
            far = out[part] * weight[h, :]
            whole = g[rows, :] + far
            dx[rows, :] = whole.astype(BF)
            x = xt_ref[rows, :].astype(F32)
            qrow[h, :] = jnp.sum(x * whole, axis=0, keepdims=True)
            q2row[h, :] = jnp.sum(x * far, axis=0, keepdims=True)
        return acc

    db_state = jnp.zeros((128, T2), F32)
    for p in range(8):
        db_state = finish(2 * p + 1, finish(2 * p, db_state))
        swap(p).start()

    def small_part():
        met = asrow[...] * tot[...]
        neg_col = jnp.broadcast_to(neg_rate, (128, 128)).T[0:HEADS, 0:1]
        for b in range(2):
            lanes = halves[b]
            mine = low if b == 0 else jnp.logical_not(low)
            end_grad = jnp.sum(jnp.where(mine, met, 0.0), axis=1, keepdims=True) + jnp.sum(
                q2row[:, lanes], axis=1, keepdims=True
            )
            dl = prow[:, lanes] - qrow[:, lanes]
            da = dot_exact(dl, tri[b]) + end_grad
            zb = zt[:, lanes]
            small_e = jnp.exp(-jnp.abs(zb))
            sig = jnp.where(zb >= 0, 1.0, small_e) / (1.0 + small_e)
            ratio = jnp.where(zb < -20.0, 1.0, sig / step_t[:, lanes])
            dz = qrow[:, lanes] * ratio + da * neg_col * sig
            dx[D + 128 : D + 160, lanes] = dz.astype(BF)
            part = slice(b * 64, b * 64 + 64)
            db = own_maps[b] + db_state[part, lanes]
            dx[D : D + 64, lanes] = db.astype(BF)
        swap(8).start()

    orders = (("z", "y", "x"), ("y", "x", "z"), ("x", "z", "y")) * 3

    def moves(p, stage):
        axis = orders[p][stage]
        here = coords[axis]
        found = []
        for k in (2, 1, 3):
            v = (here + k) % 4

            def copy_out(slot, v=v):
                if stage == 0:
                    src, dst = dec.at[pl.ds(pl.multiple_of(p * 1024 + v * 256, 256), 256), :], in1
                elif stage == 1:
                    first_row = PARTS * 1024 + p * 256
                    src, dst = dec.at[pl.ds(pl.multiple_of(first_row + v * 64, 64), 64), :], in2
                else:
                    src, dst = buf3.at[p, v], in3
                return to(
                    at_axis(axis, v), src, dst.at[p, slot],
                    ss.at[p, stage, v], rs.at[p, stage, slot],
                )

            found.append((v, lambda c=copy_out: c(here), lambda c=copy_out, v=v: c(v)))
        return found

    def launch(p, stage):
        for v, out, back in moves(p, stage):
            out().start()

    def arrived(p, stage):
        found = moves(p, stage)
        for v, out, back in found:
            back().wait_recv()
        return [v for v, out, back in found], coords[orders[p][stage]]

    def gradient(p):
        swap(p).wait_recv()
        left = jnp.concatenate(
            [ct[:, core].reshape(1024, T2), rt_in[...].reshape(1024, T2)], axis=1
        )
        right = jnp.concatenate([dx[p * COLS : (p + 1) * COLS, :], dx_in[p]], axis=1)
        tile = dot(left, right, NT).astype(BF)
        for k in range(64):
            jj, m = k // 8, k % 8
            where = {"z": m // 2, "y": jj // 2, "x": (m % 2) * 2 + jj % 2}
            a, b, d = (where[axis] for axis in orders[p])
            first_row = p * 1024 + ((a * 4 + b) * 4 + d) * 16
            dec[first_row : first_row + 16, :] = tile[k * 16 : (k + 1) * 16]
        launch(p, 0)

    def first(p):
        peers, here = arrived(p, 0)
        mine = pl.ds(pl.multiple_of(p * 1024 + here * 256, 256), 256)
        total = dec[mine, :].astype(F32)
        for v in peers:
            total = total + in1[p, v].astype(F32)
        dec[PARTS * 1024 + p * 256 : PARTS * 1024 + (p + 1) * 256, :] = total.astype(BF)
        launch(p, 1)

    def second(p):
        peers, here = arrived(p, 1)
        mine = pl.ds(pl.multiple_of(PARTS * 1024 + p * 256 + here * 64, 64), 64)
        total = dec[mine, :].astype(F32)
        for v in peers:
            total = total + in2[p, v].astype(F32)
        for v in range(4):
            buf3[p, v] = total[v * 16 : (v + 1) * 16]
        launch(p, 2)

    def third(p):
        peers, here = arrived(p, 2)
        total = buf3[p, here]
        for v in peers:
            total = total + in3[p, v]
        return total

    shares = []

    def share(kind, src, dst):
        dst[dp] = src[...]
        for k in range(1, 8):
            j = (dp + k) % 8

            def copy_out(slot, j=j):
                return to(
                    {"dp": j, "ctx": me}, src, dst.at[slot],
                    out_s.at[kind, j], out_r.at[kind, slot],
                )

            copy_out(dp).start()
            shares.append((kind, lambda c=copy_out: c(dp), lambda c=copy_out, j=j: c(j)))

    def finals(group):
        for p in (3 * group, 3 * group + 1, 3 * group + 2):
            piece = third(p)
            if p == PARTS - 1:
                last2[...] = piece
                share(3, last2, out2)
            else:
                n = p - 3 * group
                last[group, :, n * COLS : (n + 1) * COLS] = piece.astype(BF)
        share(group, last.at[group], outs.at[group])

    last[2, :, 512:768] = jnp.zeros((16, 256), BF)
    rows_swap.wait_recv()
    for p in range(4):
        gradient(p)
    small_part()
    for p in range(4, PARTS):
        gradient(p)

    for p in range(0, 6):
        first(p)
    for p in range(0, 3):
        second(p)
    for p in range(6, 9):
        first(p)
    for p in range(3, 6):
        second(p)
    finals(0)
    for p in range(6, 9):
        second(p)
    finals(1)
    finals(2)

    def gathered(kind):
        for which, out, back in shares:
            if which == kind:
                back().wait_recv()

    for kind in (0, 1, 3, 2):
        gathered(kind)
        for k in range(8):
            rows = slice(k * 16, (k + 1) * 16)
            if kind == 3:
                gs_ref[:, rows] = out2[k].T[0:160]
            else:
                width = 768 if kind < 2 else 512
                cols = slice(kind * 768, kind * 768 + width)
                gx_ref[rows, cols] = outs[kind, k][:, 0:width].astype(F32)

    sent_all(send_a, recv_a, sa, ra)
    sent_all(send_a2, recv_a2, sa2, ra2)
    sent_all(send_b, recv_b, sb, rb)
    sent_all(send_b2, recv_b2, sb2, rb2)
    rows_swap.wait_send()
    for p in range(PARTS):
        swap(p).wait_send()
        for stage in range(3):
            for v, out, back in moves(p, stage):
                out().wait_send()
    for which, out, back in shares:
        out().wait_send()


def scan(rows, x_weight, small_weight, cot, gain, log_rates, step_bias):
    vmem = pl.BlockSpec(memory_space=pltpu.VMEM)
    V = pltpu.VMEM
    dma = pltpu.SemaphoreType.DMA
    slots = [V((PEERS, SLOT, 128), BF)] * 2 + [V((PEERS, 128, 128), BF)] * 6
    return pl.pallas_call(
        scan_kernel,
        in_specs=[vmem, pl.BlockSpec(memory_space=pl.ANY)] + [vmem] * 5,
        out_specs=[vmem] * 3,
        out_shape=[
            jax.ShapeDtypeStruct((ROWS, D), BF),
            jax.ShapeDtypeStruct((128, D), F32),
            jax.ShapeDtypeStruct((160, 128), F32),
        ],
        scratch_shapes=[
            V((D, T2), BF),
            V((T2, 256), F32),
            pltpu.SemaphoreType.DMA((8,)),
            V((8, 128), F32),
            V((HEADS, T2), F32),
            V((HEADS, T2), F32),
            V((HEADS, T2), F32),
            V((HEADS, T2), F32),
            V((2, ROWS, 128), F32),
            V((HEADS, T2), F32),
            V((T2, 256), BF),
            V((256, T2), BF),
            V((T2, 256), BF),
            V((256, T2), BF),
            V((2, ROWS, ROWS), F32),
            V((2, ROWS, ROWS), F32),
            V((D, T2), BF),
            V((8, 2, 128, T2), BF),
            V((D, T2), F32),
            V((D, T2), F32),
            V((WIDE, T2), BF),
            V((D, T2), BF),
            V((2 * HEADS * ROWS, ROWS), BF),
            V((2 * HEADS * ROWS, ROWS), BF),
            V((HEADS, 128), F32),
            V((HEADS, T2), F32),
            V((HEADS, T2), F32),
            V((HEADS, T2), F32),
            V((HEADS, 128), F32),
        ]
        + slots
        + [
            V((PEERS, 128, 128), F32),
            V((8, 128, T2), BF),
            V((PARTS, COLS, T2), BF),
            V((PARTS, 4, 256, COLS), BF),
            V((PARTS, 4, 64, COLS), BF),
            V((PARTS, 4, 16, COLS), F32),
            V((PARTS, 4, 16, COLS), F32),
            V((3, 16, 768), BF),
            V((16, 256), F32),
            V((3, 8, 16, 768), BF),
            V((8, 16, 256), F32),
        ]
        + [dma((PEERS,))] * 8
        + [
            dma((PARTS + 1,)),
            dma((PARTS + 1,)),
            dma((PARTS, 3, 4)),
            dma((PARTS, 3, 4)),
            dma((4, 8)),
            dma((4, 8)),
        ],
        compiler_params=pltpu.CompilerParams(
            collective_id=0, has_side_effects=True, vmem_limit_bytes=62 * 2**20
        ),
        name="layer",
    )(rows, x_weight, small_weight, cot, gain, log_rates, step_bias)


def shards(hidden, x_weight, state_weight, log_rates, step_bias, out_gain, cotangent):
    mixed, grad_x, grad_small = scan(
        hidden[0], x_weight, state_weight.T, cotangent[0],
        out_gain[None], log_rates[None], step_bias[None],
    )
    return (mixed[None], grad_x, grad_small.T)


def solution(mesh):
    return jax.shard_map(
        shards,
        mesh=mesh,
        in_specs=(P("dp", "ctx", None), P(), P(), P(), P(), P(), P("dp", "ctx", None)),
        out_specs=(P("dp", "ctx", None), P("ctx", None), P("ctx", None)),
        check_vma=False,
    )
```

time: 146 us -> 115 us (0.79)
  Pallas kernels: 138 us -> 108 us
    pallas_call x3 -> x1, Pallas kernels: 138 us -> 108 us  [scan(): pl.pallas_call(scan_kernel, in_specs=[vmem, pl.BlockSpec(memory_space=pl....]
    unnamed x14 -> x3, local copies, waits for them, and re-layouts: 7.26 us -> 6.13 us
where the time goes in v3:
time: 115 us; the launch traced here: 114 us
  Pallas kernels  108 us (94%)
  local copies, waits for them, and re-layouts  6.13 us (5%)
    pallas_call x1, Pallas kernels, scan(): pl.pallas_call(scan_kernel, in_specs=[vmem, pl.BlockSpec(memory_space=pl....  108 us
    unnamed x3, local copies, waits for them, and re-layouts  6.13 us

profile of v3, /device:TPU:0, one launch (start us, length us, event | category | flops | bytes accessed | tf_op | source)
XLA Modules:
  0.0 114.3 jit_solution(15954113190965627679)
XLA Ops:
  0.6 107.6 %layer.1 = (bf16[256,2048]{1,0:T(8,128)(2,1)}, f32[128,2048]{1,0:T(8,128)}, f32[160,128]{1,0:T(8,128)}) custom-call(bf16[256,2048]{1,0:T(8,128)(2,1)} %bitcast.8, bf16[2048,2048]{1,0:T(8,128)(2,1)} %w_hbm.1, bf16[160,2048]{1,0:T(8,128)(2,1)} %bitcast.11, bf16[256,2048]{1,0:T(8,128)(2,1)} %bitcast.9, f32[1,2048]{1,0:T(1,128)} %bitcast.13, f32[1,32]{1,0:T(1,128)} %bitcast.14, ...), custom_call_target="tpu_custom_call" | custom-call | tf_op jit(solution)/shard_map/layer/pallas_call | solution.py:609
  108.2 2.3 %copy.13 = bf16[1,256,2048]{2,1,0:T(8,128)(2,1)} copy(bf16[1,256,2048]{2,1,0:T(8,128)(2,1)} %bitcast.10) | data formatting | bytes 2097152
  110.5 2.3 %copy.14 = f32[128,2048]{1,0:T(8,128)} copy(f32[128,2048]{1,0:T(8,128)} %get-tuple-element.13) | data formatting | bytes 2097152
  112.8 1.5 %copy.15 = f32[128,160]{0,1:T(8,128)} copy(f32[128,160]{0,1:T(8,128)} %bitcast.12) | data formatting | bytes 163840

commit v4 on v3

--- a/solution.py
+++ b/solution.py
@@ -277,12 +277,12 @@
 
         lax.fori_loop(0, PEERS, descend, zero)
 
-    lax.fori_loop(0, PAIRS // 2, forward, 0)
+    lax.fori_loop(0, PAIRS // 4, forward, 0)
     recv_all(send_a, recv_a, sa, ra)
     chain(recv_a, send_a2, True)
     recv_a2[me] = send_a2[me]
     send_all(send_a2, recv_a2, sa2, ra2)
-    lax.fori_loop(PAIRS // 2, PAIRS, forward, 0)
+    lax.fori_loop(PAIRS // 4, PAIRS, forward, 0)
 
     for blk in range(8):
         turned_c = cot_ref[:, blk * 256 : (blk + 1) * 256].T
@@ -419,12 +419,8 @@
             q2row[h, :] = jnp.sum(x * far, axis=0, keepdims=True)
         return acc
 
-    db_state = jnp.zeros((128, T2), F32)
-    for p in range(8):
-        db_state = finish(2 * p + 1, finish(2 * p, db_state))
-        swap(p).start()
-
-    def small_part():
+
+    def small_part(db_state):
         met = asrow[...] * tot[...]
         neg_col = jnp.broadcast_to(neg_rate, (128, 128)).T[0:HEADS, 0:1]
         for b in range(2):
@@ -550,13 +546,22 @@
         share(group, last.at[group], outs.at[group])
 
     last[2, :, 512:768] = jnp.zeros((16, 256), BF)
-    rows_swap.wait_recv()
-    for p in range(4):
+    db_state = jnp.zeros((128, T2), F32)
+    for p in range(8):
+        db_state = finish(2 * p + 1, finish(2 * p, db_state))
+        swap(p).start()
+        if p == 2:
+            rows_swap.wait_recv()
+        if p >= 2:
+            gradient(p - 2)
+    small_part(db_state)
+    for p in range(6, PARTS):
         gradient(p)
-    small_part()
-    for p in range(4, PARTS):
-        gradient(p)
-
+
+    sent_all(send_a, recv_a, sa, ra)
+    sent_all(send_a2, recv_a2, sa2, ra2)
+    sent_all(send_b, recv_b, sb, rb)
+    sent_all(send_b2, recv_b2, sb2, rb2)
     for p in range(0, 6):
         first(p)
     for p in range(0, 3):
@@ -587,10 +592,6 @@
                 cols = slice(kind * 768, kind * 768 + width)
                 gx_ref[rows, cols] = outs[kind, k][:, 0:width].astype(F32)
 
-    sent_all(send_a, recv_a, sa, ra)
-    sent_all(send_a2, recv_a2, sa2, ra2)
-    sent_all(send_b, recv_b, sb, rb)
-    sent_all(send_b2, recv_b2, sb2, rb2)
     rows_swap.wait_send()
     for p in range(PARTS):
         swap(p).wait_send()
@@ -676,11 +677,42 @@
     )(rows, x_weight, small_weight, cot, gain, log_rates, step_bias)
 
 
+def hand_on_kernel(*refs):
+    half = len(refs) // 2
+    sems = refs[-1]
+    pairs = list(zip(refs[:half], refs[half : 2 * half]))
+    moves = []
+    for src, dst in pairs:
+        rows = src.shape[0] // 4
+        for k in range(4):
+            part = pl.ds(k * rows, rows)
+            moves.append((src.at[part, :], dst.at[part, :]))
+    copies = [
+        pltpu.make_async_copy(src, dst, sems.at[k]) for k, (src, dst) in enumerate(moves)
+    ]
+    for c in copies:
+        c.start()
+    for c in copies:
+        c.wait()
+
+
+def hand_on(*arrays):
+    anywhere = pl.BlockSpec(memory_space=pl.ANY)
+    return pl.pallas_call(
+        hand_on_kernel,
+        in_specs=[anywhere] * len(arrays),
+        out_specs=[anywhere] * len(arrays),
+        out_shape=[jax.ShapeDtypeStruct(a.shape, a.dtype) for a in arrays],
+        scratch_shapes=[pltpu.SemaphoreType.DMA((4 * len(arrays),))],
+        name="hand_on",
+    )(*arrays)
+
+
 def shards(hidden, x_weight, state_weight, log_rates, step_bias, out_gain, cotangent):
-    mixed, grad_x, grad_small = scan(
+    mixed, grad_x, grad_small = hand_on(*scan(
         hidden[0], x_weight, state_weight.T, cotangent[0],
         out_gain[None], log_rates[None], step_bias[None],
-    )
+    ))
     return (mixed[None], grad_x, grad_small.T)
 
 

time: 115 us -> 173 us (1.50)
  Pallas kernels: 108 us -> 172 us
  local copies, waits for them, and re-layouts: 6.13 us -> 0 us
    pallas_call x0 -> x1, Pallas kernels: none -> 67.2 us  [hand_on(): pl.pallas_call(hand_on_kernel, in_specs=[anywhere] * len(arrays), out_spe...]
    unnamed x3 -> x0, local copies, waits for them, and re-layouts: 6.13 us -> none
    pallas_call x1, Pallas kernels: 108 us -> 105 us  [scan(): pl.pallas_call(scan_kernel, in_specs=[vmem, pl.BlockSpec(memory_space=pl....]
where the time goes in v4:
time: 173 us
  Pallas kernels  172 us (99%)
    pallas_call x1, Pallas kernels, scan(): pl.pallas_call(scan_kernel, in_specs=[vmem, pl.BlockSpec(memory_space=pl....  105 us
    pallas_call x1, Pallas kernels, hand_on(): pl.pallas_call(hand_on_kernel, in_specs=[anywhere] * len(arrays), out_spe...  67.2 us

profile of v4, /device:TPU:0, one launch (start us, length us, event | category | flops | bytes accessed | tf_op | source)
XLA Modules:
  0.0 172.6 jit_solution(13593565606554245696)
XLA Ops:
  0.6 104.6 %layer.1 = (bf16[256,2048]{1,0:T(8,128)(2,1)}, f32[128,2048]{1,0:T(8,128)}, f32[160,128]{1,0:T(8,128)}) custom-call(bf16[256,2048]{1,0:T(8,128)(2,1)} %bitcast.8, bf16[2048,2048]{1,0:T(8,128)(2,1)} %w_hbm.1, bf16[160,2048]{1,0:T(8,128)(2,1)} %bitcast.10, bf16[256,2048]{1,0:T(8,128)(2,1)} %bitcast.9, f32[1,2048]{1,0:T(1,128)} %bitcast.11, f32[1,32]{1,0:T(1,128)} %bitcast.12, ...), custom_call_target="tpu_custom_call" | custom-call | tf_op jit(solution)/shard_map/layer/pallas_call | solution.py:610
  105.2 67.2 %hand_on.1 = (bf16[256,2048]{1,0:T(8,128)(2,1)}, f32[128,2048]{1,0:T(8,128)}, f32[160,128]{1,0:T(8,128)}) custom-call(bf16[256,2048]{1,0:T(8,128)(2,1)} %get-tuple-element.9.refs_0_, f32[128,2048]{1,0:T(8,128)} %get-tuple-element.10.refs_1_, f32[160,128]{1,0:T(8,128)} %get-tuple-element.11.refs_2_), custom_call_target="tpu_custom_call" | custom-call | tf_op jit(solution)/shard_map/hand_on/pallas_call | solution.py:701

commit v5 on v4

--- a/solution.py
+++ b/solution.py
@@ -52,7 +52,7 @@
     small, zt, step_t, weight, l2_t, l2_n, el_t, bdb, bdbt, bdc, bdct, scm, dsc,
     wx, ct, u, g, du, vdu, mst, dec, tot, prow, qrow, q2row, asrow,
     send_a, recv_a, send_a2, recv_a2, send_b, recv_b, send_b2, recv_b2, up,
-    rt_in, dx_in, in1, in2, buf3, in3, last, last2, outs, out2,
+    rt_in, dx_in, in1, in2, buf3, in3, last0, last1, outs0, outs1,
     sa, ra, sa2, ra2, sb, rb, sb2, rb2, core_s, core_r, ss, rs, out_s, out_r,
 ):
     me = lax.axis_index("ctx")
@@ -534,18 +534,17 @@
             copy_out(dp).start()
             shares.append((kind, lambda c=copy_out: c(dp), lambda c=copy_out, j=j: c(j)))
 
-    def finals(group):
-        for p in (3 * group, 3 * group + 1, 3 * group + 2):
+    def finals(parts):
+        for p in parts:
             piece = third(p)
+            whole = piece.astype(BF)
+            if p < 6:
+                last0[:, p * COLS : (p + 1) * COLS] = whole
+            else:
+                last1[:, (p - 6) * COLS : (p - 5) * COLS] = whole
             if p == PARTS - 1:
-                last2[...] = piece
-                share(3, last2, out2)
-            else:
-                n = p - 3 * group
-                last[group, :, n * COLS : (n + 1) * COLS] = piece.astype(BF)
-        share(group, last.at[group], outs.at[group])
-
-    last[2, :, 512:768] = jnp.zeros((16, 256), BF)
+                last1[:, 3 * COLS : 4 * COLS] = (piece - whole.astype(F32)).astype(BF)
+
     db_state = jnp.zeros((128, T2), F32)
     for p in range(8):
         db_state = finish(2 * p + 1, finish(2 * p, db_state))
@@ -570,27 +569,27 @@
         first(p)
     for p in range(3, 6):
         second(p)
-    finals(0)
     for p in range(6, 9):
         second(p)
-    finals(1)
-    finals(2)
+    finals(range(0, 6))
+    share(0, last0, outs0)
+    finals(range(6, 9))
+    share(1, last1, outs1)
 
     def gathered(kind):
         for which, out, back in shares:
             if which == kind:
                 back().wait_recv()
 
-    for kind in (0, 1, 3, 2):
-        gathered(kind)
-        for k in range(8):
-            rows = slice(k * 16, (k + 1) * 16)
-            if kind == 3:
-                gs_ref[:, rows] = out2[k].T[0:160]
-            else:
-                width = 768 if kind < 2 else 512
-                cols = slice(kind * 768, kind * 768 + width)
-                gx_ref[rows, cols] = outs[kind, k][:, 0:width].astype(F32)
+    gathered(0)
+    for k in range(8):
+        gx_ref[k * 16 : (k + 1) * 16, 0:1536] = outs0[k].astype(F32)
+    gathered(1)
+    for k in range(8):
+        rows = slice(k * 16, (k + 1) * 16)
+        gx_ref[rows, 1536:D] = outs1[k, :, 0:512].astype(F32)
+        narrow = outs1[k, :, 512:768].astype(F32) + outs1[k, :, 768:1024].astype(F32)
+        gs_ref[:, rows] = narrow.T[0:160]
 
     rows_swap.wait_send()
     for p in range(PARTS):
@@ -656,10 +655,10 @@
             V((PARTS, 4, 64, COLS), BF),
             V((PARTS, 4, 16, COLS), F32),
             V((PARTS, 4, 16, COLS), F32),
-            V((3, 16, 768), BF),
-            V((16, 256), F32),
-            V((3, 8, 16, 768), BF),
-            V((8, 16, 256), F32),
+            V((16, 1536), BF),
+            V((16, 1024), BF),
+            V((8, 16, 1536), BF),
+            V((8, 16, 1024), BF),
         ]
         + [dma((PEERS,))] * 8
         + [
@@ -667,8 +666,8 @@
             dma((PARTS + 1,)),
             dma((PARTS, 3, 4)),
             dma((PARTS, 3, 4)),
-            dma((4, 8)),
-            dma((4, 8)),
+            dma((2, 8)),
+            dma((2, 8)),
         ],
         compiler_params=pltpu.CompilerParams(
             collective_id=0, has_side_effects=True, vmem_limit_bytes=62 * 2**20
@@ -678,32 +677,38 @@
 
 
 def hand_on_kernel(*refs):
-    half = len(refs) // 2
-    sems = refs[-1]
-    pairs = list(zip(refs[:half], refs[half : 2 * half]))
-    moves = []
-    for src, dst in pairs:
+    count = (len(refs) - 2) // 3
+    ins, outs, held = refs[:count], refs[count : 2 * count], refs[2 * count : 3 * count]
+    read_sem, write_sem = refs[3 * count :]
+    chunks = []
+    for src, dst, buf in zip(ins, outs, held):
         rows = src.shape[0] // 4
         for k in range(4):
             part = pl.ds(k * rows, rows)
-            moves.append((src.at[part, :], dst.at[part, :]))
-    copies = [
-        pltpu.make_async_copy(src, dst, sems.at[k]) for k, (src, dst) in enumerate(moves)
-    ]
-    for c in copies:
-        c.start()
-    for c in copies:
-        c.wait()
+            i = len(chunks)
+            chunks.append((
+                pltpu.make_async_copy(src.at[part, :], buf.at[part, :], read_sem.at[i]),
+                pltpu.make_async_copy(buf.at[part, :], dst.at[part, :], write_sem.at[i]),
+            ))
+    for read, write in chunks:
+        read.start()
+    for read, write in chunks:
+        read.wait()
+        write.start()
+    for read, write in chunks:
+        write.wait()
 
 
 def hand_on(*arrays):
     anywhere = pl.BlockSpec(memory_space=pl.ANY)
+    dma = pltpu.SemaphoreType.DMA
     return pl.pallas_call(
         hand_on_kernel,
         in_specs=[anywhere] * len(arrays),
         out_specs=[anywhere] * len(arrays),
         out_shape=[jax.ShapeDtypeStruct(a.shape, a.dtype) for a in arrays],
-        scratch_shapes=[pltpu.SemaphoreType.DMA((4 * len(arrays),))],
+        scratch_shapes=[pltpu.VMEM(a.shape, a.dtype) for a in arrays]
+        + [dma((4 * len(arrays),)), dma((4 * len(arrays),))],
         name="hand_on",
     )(*arrays)
 

time: 173 us -> 110 us (0.64); the launches traced: 173 us -> 108 us
  Pallas kernels: 172 us -> 107 us
    pallas_call x1, Pallas kernels: 67.2 us -> 2.48 us  [hand_on(): pl.pallas_call(hand_on_kernel, in_specs=[anywhere] * len(arrays), out_spe...]
where the time goes in v5:
time: 110 us; the launch traced here: 108 us
  Pallas kernels  107 us (97%)
    pallas_call x1, Pallas kernels, scan(): pl.pallas_call(scan_kernel, in_specs=[vmem, pl.BlockSpec(memory_space=pl....  104 us
    pallas_call x1, Pallas kernels, hand_on(): pl.pallas_call(hand_on_kernel, in_specs=[anywhere] * len(arrays), out_spe...  2.48 us

profile of v5, /device:TPU:0, one launch (start us, length us, event | category | flops | bytes accessed | tf_op | source)
XLA Modules:
  0.0 107.6 jit_solution(3132379260108661334)
XLA Ops:
  0.6 104.3 %layer.1 = (bf16[256,2048]{1,0:T(8,128)(2,1)}, f32[128,2048]{1,0:T(8,128)}, f32[160,128]{1,0:T(8,128)}) custom-call(bf16[256,2048]{1,0:T(8,128)(2,1)} %bitcast.8, bf16[2048,2048]{1,0:T(8,128)(2,1)} %w_hbm.1, bf16[160,2048]{1,0:T(8,128)(2,1)} %bitcast.10, bf16[256,2048]{1,0:T(8,128)(2,1)} %bitcast.9, f32[1,2048]{1,0:T(1,128)} %bitcast.11, f32[1,32]{1,0:T(1,128)} %bitcast.12, ...), custom_call_target="tpu_custom_call" | custom-call | tf_op jit(solution)/shard_map/layer/pallas_call | solution.py:609
  104.9 2.5 %hand_on.1 = (bf16[256,2048]{1,0:T(8,128)(2,1)}, f32[128,2048]{1,0:T(8,128)}, f32[160,128]{1,0:T(8,128)}) custom-call(bf16[256,2048]{1,0:T(8,128)(2,1)} %get-tuple-element.9.refs_0_, f32[128,2048]{1,0:T(8,128)} %get-tuple-element.10.refs_1_, f32[160,128]{1,0:T(8,128)} %get-tuple-element.11.refs_2_), custom_call_target="tpu_custom_call" | custom-call | tf_op jit(solution)/shard_map/hand_on/pallas_call | solution.py:705

commit v6 on v5

--- a/solution.py
+++ b/solution.py
@@ -556,12 +556,13 @@
     small_part(db_state)
     for p in range(6, PARTS):
         gradient(p)
+        first(p - 6)
 
     sent_all(send_a, recv_a, sa, ra)
     sent_all(send_a2, recv_a2, sa2, ra2)
     sent_all(send_b, recv_b, sb, rb)
     sent_all(send_b2, recv_b2, sb2, rb2)
-    for p in range(0, 6):
+    for p in range(3, 6):
         first(p)
     for p in range(0, 3):
         second(p)

time: 110 us -> 107 us (0.973); the launches traced: 108 us -> 107 us
  no operation moved by 1% of the time
where the time goes in v6:
time: 107 us
  Pallas kernels  106 us (99%)
    pallas_call x1, Pallas kernels, scan(): pl.pallas_call(scan_kernel, in_specs=[vmem, pl.BlockSpec(memory_space=pl....  104 us
    pallas_call x1, Pallas kernels, hand_on(): pl.pallas_call(hand_on_kernel, in_specs=[anywhere] * len(arrays), out_spe...  2.48 us

profile of v6, /device:TPU:0, one launch (start us, length us, event | category | flops | bytes accessed | tf_op | source)
XLA Modules:
  0.0 106.8 jit_solution(12294535559183906445)
XLA Ops:
  0.6 103.5 %layer.1 = (bf16[256,2048]{1,0:T(8,128)(2,1)}, f32[128,2048]{1,0:T(8,128)}, f32[160,128]{1,0:T(8,128)}) custom-call(bf16[256,2048]{1,0:T(8,128)(2,1)} %bitcast.8, bf16[2048,2048]{1,0:T(8,128)(2,1)} %w_hbm.1, bf16[160,2048]{1,0:T(8,128)(2,1)} %bitcast.10, bf16[256,2048]{1,0:T(8,128)(2,1)} %bitcast.9, f32[1,2048]{1,0:T(1,128)} %bitcast.11, f32[1,32]{1,0:T(1,128)} %bitcast.12, ...), custom_call_target="tpu_custom_call" | custom-call | tf_op jit(solution)/shard_map/layer/pallas_call | solution.py:610
  104.2 2.5 %hand_on.1 = (bf16[256,2048]{1,0:T(8,128)(2,1)}, f32[128,2048]{1,0:T(8,128)}, f32[160,128]{1,0:T(8,128)}) custom-call(bf16[256,2048]{1,0:T(8,128)(2,1)} %get-tuple-element.9.refs_0_, f32[128,2048]{1,0:T(8,128)} %get-tuple-element.10.refs_1_, f32[160,128]{1,0:T(8,128)} %get-tuple-element.11.refs_2_), custom_call_target="tpu_custom_call" | custom-call | tf_op jit(solution)/shard_map/hand_on/pallas_call | solution.py:706

commit v7 on v6

--- a/solution.py
+++ b/solution.py
@@ -356,7 +356,7 @@
                 dsc[b, span(i), span(j)] = acc
         return c
 
-    lax.fori_loop(0, PAIRS // 2, backward, 0)
+    lax.fori_loop(0, 10, backward, 0)
     for blk in range(8):
         y_rc = u[(7 - blk) * 256 : (8 - blk) * 256, ROWS:T2].astype(BF)
         y = u[blk * 256 : (blk + 1) * 256, 0:ROWS] + dot(flip, y_rc)
@@ -370,7 +370,7 @@
     chain(recv_b, send_b2, False)
     recv_b2[me] = send_b2[me]
     send_all(send_b2, recv_b2, sb2, rb2)
-    lax.fori_loop(PAIRS // 2, PAIRS, backward, 0)
+    lax.fori_loop(10, PAIRS, backward, 0)
 
     own_maps = []
     for b in range(2):

time: 107 us -> 108 us (level)
  no operation moved by 1% of the time
where the time goes in v7:
time: 108 us
  Pallas kernels  107 us (99%)
    pallas_call x1, Pallas kernels, scan(): pl.pallas_call(scan_kernel, in_specs=[vmem, pl.BlockSpec(memory_space=pl....  104 us
    pallas_call x1, Pallas kernels, hand_on(): pl.pallas_call(hand_on_kernel, in_specs=[anywhere] * len(arrays), out_spe...  2.48 us

profile of v7, /device:TPU:0, one launch (start us, length us, event | category | flops | bytes accessed | tf_op | source)
XLA Modules:
  0.0 107.6 jit_solution(9952120857714969091)
XLA Ops:
  0.6 104.3 %layer.1 = (bf16[256,2048]{1,0:T(8,128)(2,1)}, f32[128,2048]{1,0:T(8,128)}, f32[160,128]{1,0:T(8,128)}) custom-call(bf16[256,2048]{1,0:T(8,128)(2,1)} %bitcast.8, bf16[2048,2048]{1,0:T(8,128)(2,1)} %w_hbm.1, bf16[160,2048]{1,0:T(8,128)(2,1)} %bitcast.10, bf16[256,2048]{1,0:T(8,128)(2,1)} %bitcast.9, f32[1,2048]{1,0:T(1,128)} %bitcast.11, f32[1,32]{1,0:T(1,128)} %bitcast.12, ...), custom_call_target="tpu_custom_call" | custom-call | tf_op jit(solution)/shard_map/layer/pallas_call | solution.py:610
  104.9 2.5 %hand_on.1 = (bf16[256,2048]{1,0:T(8,128)(2,1)}, f32[128,2048]{1,0:T(8,128)}, f32[160,128]{1,0:T(8,128)}) custom-call(bf16[256,2048]{1,0:T(8,128)(2,1)} %get-tuple-element.9.refs_0_, f32[128,2048]{1,0:T(8,128)} %get-tuple-element.10.refs_1_, f32[160,128]{1,0:T(8,128)} %get-tuple-element.11.refs_2_), custom_call_target="tpu_custom_call" | custom-call | tf_op jit(solution)/shard_map/hand_on/pallas_call | solution.py:706
